TPU v7x, 128 devices: a whole 4x4x4 slice. The times are simulated.
128 devices in a mesh: dp: 32 (over z, x, core), section: 4 (over y).
Axes of the slice: x: 4, y: 4, z: 4, core: 2. Of those that a mesh axis runs over, the one named last changes fastest.
Arguments:
- tokens: bfloat16 [64, 256, 768], P('dp'), may hold values from -6 to 6
- cotangent: bfloat16 [64, 256, 768], P('dp'), may hold values from -6 to 6
- page_numbers: int32 [64, 256], P('dp'), may hold values from 0 to 7, never falling along the last dimension, each value on 1 to 128 neighbouring positions
- offset_bucket: int32 [511], replicated, may hold values from 0 to 31
- attend_gain: float32 [2, 768], replicated, may hold values from 0.5 to 1.5
- attend_shift: float32 [2, 768], replicated, may hold values from -1.5 to 1.5
- input_weight: bfloat16 [2, 768, 2304], replicated, may hold values from -0.21875 to 0.21875
- query_bias: float32 [2, 768], replicated, may hold values from -1.5 to 1.5
- value_bias: float32 [2, 768], replicated, may hold values from -1.5 to 1.5
- bias_table: float32 [2, 12, 32], replicated, may hold values from -4 to 4
- output_weight: bfloat16 [2, 768, 768], replicated, may hold values from -0.625 to 0.625
- output_bias: float32 [2, 768], replicated, may hold values from -1.5 to 1.5
- attend_scale: float32 [2, 768], replicated, may hold values from 0.5 to 2
- forward_gain: float32 [2, 768], replicated, may hold values from 0.5 to 1.5
- forward_shift: float32 [2, 768], replicated, may hold values from -1.5 to 1.5
- upward_weight: bfloat16 [2, 768, 3072], replicated, may hold values from -0.21875 to 0.21875
- upward_bias: float32 [2, 3072], replicated, may hold values from -1.5 to 1.5
- downward_weight: bfloat16 [2, 3072, 768], replicated, may hold values from -0.109375 to 0.109375
- downward_bias: float32 [2, 768], replicated, may hold values from -1.5 to 1.5
- forward_scale: float32 [2, 768], replicated, may hold values from 0.5 to 2
Outputs:
- section_outputs: bfloat16 [4, 64, 256, 768], P('section', 'dp')
- input_gradients: bfloat16 [4, 64, 256, 768], P('section', 'dp')
- attend_gain_gradient: float32 [2, 768], P(None, 'dp')
- attend_shift_gradient: float32 [2, 768], P(None, 'dp')
- input_weight_gradient: float32 [2, 768, 2304], P(None, 'dp')
- query_bias_gradient: float32 [2, 768], P(None, 'dp')
- value_bias_gradient: float32 [2, 768], P(None, 'dp')
- bias_table_gradient: float32 [2, 12, 32], replicated
- output_weight_gradient: float32 [2, 768, 768], P(None, 'dp')
- output_bias_gradient: float32 [2, 768], P(None, 'dp')
- attend_scale_gradient: float32 [2, 768], P(None, 'dp')
- forward_gain_gradient: float32 [2, 768], P(None, 'dp')
- forward_shift_gradient: float32 [2, 768], P(None, 'dp')
- upward_weight_gradient: float32 [2, 768, 3072], P(None, 'dp')
- upward_bias_gradient: float32 [2, 3072], P(None, 'dp')
- downward_weight_gradient: float32 [2, 3072, 768], P(None, 'dp')
- downward_bias_gradient: float32 [2, 768], P(None, 'dp')
- forward_scale_gradient: float32 [2, 768], P(None, 'dp')
Inputs may be any that keep to these rules, and one draw needn't show every extreme that they name: `page_numbers`: in each row page numbers never fall and take every value from 0 to 7; a page covers at most 128 positions.
All inputs are finite; a program needn't handle non-finite values.
Results may differ from a plain program's by a relative error of at most 0.017.
Values may be sent and summed in bfloat16 or wider, within the bound.
A program may use at most 256 MiB of HBM per device.

v0:
```python
import jax
import jax.numpy as jnp
from jax import lax
from jax.sharding import PartitionSpec as P

EPSILON = 1e-05
NEGATIVE = -1e30


def from_behind(shard, axis, by):
    devices = lax.axis_size(axis)
    pairs = [(i, i + by) for i in range(devices) if 0 <= i + by < devices]
    return lax.ppermute(shard, axis, pairs)


def transposed_dot(left, right):
    return lax.dot_general(
        left, right, (((0,), (0,)), ((), ())), preferred_element_type=jnp.float32
    )


def right_dot(left, right):
    return lax.dot_general(
        left, right, (((1,), (1,)), ((), ())), preferred_element_type=jnp.float32
    )


def normalize(hidden):
    center = hidden - jnp.mean(hidden, axis=-1, keepdims=True)
    inv_std = lax.rsqrt(jnp.mean(center * center, axis=-1, keepdims=True) + EPSILON)
    return (center * inv_std, inv_std)


def normalize_back(upstream, normed, inv_std, gain):
    scaled = upstream * gain
    return inv_std * (
        scaled
        - jnp.mean(scaled, axis=-1, keepdims=True)
        - normed * jnp.mean(scaled * normed, axis=-1, keepdims=True)
    )


def expand_offsets(offset_bias, rows, length):
    heads = offset_bias.shape[0]
    width = rows + length - 1
    tiled = jnp.broadcast_to(offset_bias[:, None, :], (heads, rows, width)).reshape(
        heads, rows * width
    )
    sheared = jnp.pad(tiled, ((0, 0), (0, rows))).reshape(heads, rows, width + 1)[:, :, :length]
    return sheared[:, ::-1, :]


def fold_offsets(grad_scores, rows, length):
    heads = grad_scores.shape[0]
    width = rows + length - 1
    flipped = grad_scores[:, ::-1, :]
    padded = jnp.pad(flipped, ((0, 0), (0, 0), (0, rows))).reshape(heads, rows * (width + 1))
    sheared = padded[:, : rows * width].reshape(heads, rows, width)
    summed = jnp.sum(sheared, axis=1)
    return summed


def block_scores(query_rows, key_heads, bias_rows, pages, start, rows, factor):
    raw = jnp.einsum("qhd,khd->hqk", query_rows, key_heads, preferred_element_type=jnp.float32)
    scores = raw * factor + bias_rows
    same = pages[start : start + rows, None] == pages[None, :]
    return jnp.where(same[None], scores, NEGATIVE)


def attend_core(hidden, weights, pages, bias_full):
    gain, shift, input_weight, query_bias, value_bias, output_weight, output_bias, scale = weights
    length, width = hidden.shape
    heads = bias_full.shape[0]
    size = width // heads
    factor = size ** (-0.5)
    normed, inv_std = normalize(hidden)
    lowered = (normed * gain + shift).astype(jnp.bfloat16)
    project = jnp.dot(lowered, input_weight, preferred_element_type=jnp.float32)
    queries = (project[:, :width] + query_bias).astype(jnp.bfloat16).reshape(length, heads, size)
    key_heads = project[:, width : 2 * width].astype(jnp.bfloat16).reshape(length, heads, size)
    value_heads = (
        (project[:, 2 * width :] + value_bias).astype(jnp.bfloat16).reshape(length, heads, size)
    )
    rows = min(length, 512)
    scores = block_scores(queries, key_heads, bias_full, pages, 0, rows, factor)
    top = jnp.max(scores, axis=-1, keepdims=True)
    expo = jnp.exp(scores - top)
    total = jnp.sum(expo, axis=-1, keepdims=True)
    probability = (expo / total).astype(jnp.bfloat16)
    pieces = [
        jnp.einsum("hqk,khd->qhd", probability, value_heads, preferred_element_type=jnp.float32)
    ]
    sums = [top + jnp.log(total)]
    mixed = jnp.concatenate(pieces, axis=0).reshape(length, width).astype(jnp.bfloat16)
    return (normed, inv_std, lowered, queries, key_heads, value_heads, sums, mixed)


def attend_all(hidden, weights, pages, bias_full):
    output_weight, output_bias, scale = (weights[5], weights[6], weights[7])
    mixed = attend_core(hidden, weights, pages, bias_full)[7]
    branch = jnp.dot(mixed, output_weight, preferred_element_type=jnp.float32) + output_bias
    return ((hidden + scale * branch).astype(jnp.bfloat16), branch)


def attend_back(upstream, hidden, branch, weights, pages, bias_full):
    gain, shift, input_weight, query_bias, value_bias, output_weight, output_bias, scale = weights
    normed, inv_std, lowered, queries, key_heads, value_heads, sums, mixed = attend_core(
        hidden, weights, pages, bias_full
    )
    length, width = hidden.shape
    heads = bias_full.shape[0]
    size = width // heads
    factor = size ** (-0.5)
    rows = min(length, 512)
    grad_branch = (upstream * scale).astype(jnp.bfloat16)
    scale_grad = jnp.sum(upstream * branch, axis=0)
    outbias_grad = jnp.sum(grad_branch.astype(jnp.float32), axis=0)
    outweight_grad = transposed_dot(mixed, grad_branch)
    grad_mixed = (
        right_dot(grad_branch, output_weight).astype(jnp.bfloat16).reshape(length, heads, size)
    )
    grad_keys = jnp.zeros((length, heads, size), jnp.float32)
    grad_values = jnp.zeros((length, heads, size), jnp.float32)
    grad_rows = []
    score_rows = []
    for number, start in enumerate(range(0, length, rows)):
        scores = block_scores(queries, key_heads, bias_full, pages, start, rows, factor)
        probability = jnp.exp(scores - sums[number])
        grad_prob = jnp.einsum(
            "qhd,khd->hqk", grad_mixed, value_heads, preferred_element_type=jnp.float32
        )
        inner = jnp.sum(grad_prob * probability, axis=-1, keepdims=True)
        grad_scores = (probability * (grad_prob - inner)).astype(jnp.bfloat16)
        grad_values = grad_values + jnp.einsum(
            "hqk,qhd->khd",
            probability.astype(jnp.bfloat16),
            grad_mixed,
            preferred_element_type=jnp.float32,
        )
        grad_rows.append(
            jnp.einsum("hqk,khd->qhd", grad_scores, key_heads, preferred_element_type=jnp.float32)
            * factor
        )
        grad_keys = (
            grad_keys
            + jnp.einsum("hqk,qhd->khd", grad_scores, queries, preferred_element_type=jnp.float32)
            * factor
        )
        score_rows.append(grad_scores.astype(jnp.float32))
    score_grad = jnp.concatenate(score_rows, axis=1)
    grad_queries = jnp.concatenate(grad_rows, axis=0).reshape(length, width).astype(jnp.bfloat16)
    grad_keys_low = grad_keys.reshape(length, width).astype(jnp.bfloat16)
    grad_values_low = grad_values.reshape(length, width).astype(jnp.bfloat16)
    qbias_grad = jnp.sum(grad_queries.astype(jnp.float32), axis=0)
    vbias_grad = jnp.sum(grad_values_low.astype(jnp.float32), axis=0)
    grad_project = jnp.concatenate([grad_queries, grad_keys_low, grad_values_low], axis=1)
    inweight_grad = transposed_dot(lowered, grad_project)
    grad_lowered = right_dot(grad_project, input_weight)
    gain_grad = jnp.sum(grad_lowered * normed, axis=0)
    shift_grad = jnp.sum(grad_lowered, axis=0)
    grad_hidden = upstream + normalize_back(grad_lowered, normed, inv_std, gain)
    parts = (
        gain_grad,
        shift_grad,
        inweight_grad,
        qbias_grad,
        vbias_grad,
        outweight_grad,
        outbias_grad,
        scale_grad,
    )
    return (grad_hidden.astype(jnp.bfloat16), parts, score_grad)


def feed_core(hidden, weights):
    gain, shift, upward_weight, upward_bias = (weights[0], weights[1], weights[2], weights[3])
    normed, inv_std = normalize(hidden)
    lowered = (normed * gain + shift).astype(jnp.bfloat16)
    before = jnp.dot(lowered, upward_weight, preferred_element_type=jnp.float32) + upward_bias
    after = jax.nn.gelu(before, approximate=True).astype(jnp.bfloat16)
    return (normed, inv_std, lowered, before, after)


def feed_all(hidden, weights):
    downward_weight, downward_bias, scale = (weights[4], weights[5], weights[6])
    after = feed_core(hidden, weights)[4]
    branch = jnp.dot(after, downward_weight, preferred_element_type=jnp.float32) + downward_bias
    return ((hidden + scale * branch).astype(jnp.bfloat16), branch)


def feed_back(upstream, hidden, branch, weights):
    gain, shift, upward_weight, upward_bias, downward_weight, downward_bias, scale = weights
    normed, inv_std, lowered, before, after = feed_core(hidden, weights)
    grad_branch = (upstream * scale).astype(jnp.bfloat16)
    scale_grad = jnp.sum(upstream * branch, axis=0)
    dbias_grad = jnp.sum(grad_branch.astype(jnp.float32), axis=0)
    dweight_grad = transposed_dot(after, grad_branch)
    grad_after = right_dot(grad_branch, downward_weight)

    def activation(value):
        return jax.nn.gelu(value, approximate=True)

    unused, pullback = jax.vjp(activation, before)
    grad_before = pullback(grad_after)[0].astype(jnp.bfloat16)
    ubias_grad = jnp.sum(grad_before.astype(jnp.float32), axis=0)
    uweight_grad = transposed_dot(lowered, grad_before)
    grad_lowered = right_dot(grad_before, upward_weight)
    gain_grad = jnp.sum(grad_lowered * normed, axis=0)
    shift_grad = jnp.sum(grad_lowered, axis=0)
    grad_hidden = upstream + normalize_back(grad_lowered, normed, inv_std, gain)
    parts = (gain_grad, shift_grad, uweight_grad, ubias_grad, dweight_grad, dbias_grad, scale_grad)
    return (grad_hidden.astype(jnp.bfloat16), parts)


def put_slot(array, value, slot, valid):
    old = lax.dynamic_index_in_dim(array, slot, 0, keepdims=False)
    return lax.dynamic_update_index_in_dim(array, jnp.where(valid, value, old), slot, 0)


def body(
    tokens,
    cotangent,
    page_numbers,
    offset_bucket,
    attend_gain,
    attend_shift,
    input_weight,
    query_bias,
    value_bias,
    bias_table,
    output_weight,
    output_bias,
    attend_scale,
    forward_gain,
    forward_shift,
    upward_weight,
    upward_bias,
    downward_weight,
    downward_bias,
    forward_scale,
):
    section = lax.axis_index("section")
    depth = lax.axis_size("section")
    kind = section % 2
    layer = section // 2
    batches, length, width = tokens.shape
    buckets = bias_table.shape[2]

    def pick(array):
        return lax.dynamic_index_in_dim(array, layer, 0, keepdims=False)

    attend_weights = (
        pick(attend_gain),
        pick(attend_shift),
        pick(input_weight),
        pick(query_bias),
        pick(value_bias),
        pick(output_weight),
        pick(output_bias),
        pick(attend_scale),
    )
    feed_weights = (
        pick(forward_gain),
        pick(forward_shift),
        pick(upward_weight),
        pick(upward_bias),
        pick(downward_weight),
        pick(downward_bias),
        pick(forward_scale),
    )
    selector = (jnp.arange(buckets, dtype=jnp.int32)[:, None] == offset_bucket[None, :]).astype(
        jnp.float32
    )
    offset_bias = jnp.dot(pick(bias_table), selector, precision=lax.Precision.HIGHEST)
    bias_full = expand_offsets(offset_bias, length, length)
    blank = jnp.zeros((length, width), jnp.bfloat16)
    blank_wide = jnp.zeros((length, width), jnp.float32)

    def attend_forward(given, pages):
        return attend_all(given.astype(jnp.float32), attend_weights, pages, bias_full)

    def feed_forward(given, pages):
        return feed_all(given.astype(jnp.float32), feed_weights)

    def run_forward(given, pages):
        return lax.cond(kind == 0, attend_forward, feed_forward, given, pages)

    def skip_forward(given, pages):
        return (blank, blank_wide)

    received = blank
    stored = jnp.zeros((batches, length, width), jnp.bfloat16)
    outputs = stored
    branches = jnp.zeros((batches, length, width), jnp.float32)
    for tick in range(batches + depth - 1):
        index = tick - section
        valid = (index >= 0) & (index < batches)
        slot = jnp.clip(index, 0, batches - 1)
        first = lax.dynamic_index_in_dim(tokens, slot, 0, keepdims=False)
        given = jnp.where(section == 0, first, received)
        pages = lax.dynamic_index_in_dim(page_numbers, slot, 0, keepdims=False)
        result, branch = lax.cond(valid, run_forward, skip_forward, given, pages)
        stored = put_slot(stored, given, slot, valid)
        outputs = put_slot(outputs, result, slot, valid)
        branches = put_slot(branches, branch, slot, valid)
        received = from_behind(result, "section", 1)

    def back_attend(upstream, given, branch, pages, state):
        attend_total, offset_total, feed_total = state
        sent, parts, score_grad = attend_back(
            upstream.astype(jnp.float32),
            given.astype(jnp.float32),
            branch,
            attend_weights,
            pages,
            bias_full,
        )
        return (
            sent,
            (jax.tree.map(jnp.add, attend_total, parts), offset_total + score_grad, feed_total),
        )

    def back_feed(upstream, given, branch, pages, state):
        attend_total, offset_total, feed_total = state
        sent, parts = feed_back(
            upstream.astype(jnp.float32), given.astype(jnp.float32), branch, feed_weights
        )
        return (sent, (attend_total, offset_total, jax.tree.map(jnp.add, feed_total, parts)))

    def run_backward(upstream, given, branch, pages, state):
        return lax.cond(kind == 0, back_attend, back_feed, upstream, given, branch, pages, state)

    def skip_backward(upstream, given, branch, pages, state):
        return (blank, state)

    state = (
        tuple((jnp.zeros_like(array, dtype=jnp.float32) for array in attend_weights)),
        jnp.zeros_like(bias_full),
        tuple((jnp.zeros_like(array, dtype=jnp.float32) for array in feed_weights)),
    )
    received = blank
    gradients = jnp.zeros((batches, length, width), jnp.bfloat16)
    for tick in range(batches + depth - 1):
        index = tick - (depth - 1 - section)
        valid = (index >= 0) & (index < batches)
        slot = jnp.clip(index, 0, batches - 1)
        last = lax.dynamic_index_in_dim(cotangent, slot, 0, keepdims=False)
        upstream = jnp.where(section == depth - 1, last, received)
        given = lax.dynamic_index_in_dim(stored, slot, 0, keepdims=False)
        branch = lax.dynamic_index_in_dim(branches, slot, 0, keepdims=False)
        pages = lax.dynamic_index_in_dim(page_numbers, slot, 0, keepdims=False)
        sent, state = lax.cond(
            valid, run_backward, skip_backward, upstream, given, branch, pages, state
        )
        gradients = put_slot(gradients, sent, slot, valid)
        received = from_behind(sent, "section", -1)
    attend_total, offset_total, feed_total = state
    a_gain, a_shift, a_input, a_query, a_value, a_output, a_obias, a_scale = attend_total
    f_gain, f_shift, f_upward, f_ubias, f_downward, f_dbias, f_scale = feed_total
    first_flag = (layer == 0).astype(jnp.float32)
    second_flag = (layer == 1).astype(jnp.float32)
    offset_grad = fold_offsets(offset_total, length, length)
    table_grad = lax.dot_general(
        offset_grad,
        selector,
        (((1,), (1,)), ((), ())),
        precision=lax.Precision.HIGHEST,
        preferred_element_type=jnp.float32,
    )
    table_slots = jnp.stack([table_grad * first_flag, table_grad * second_flag])
    table_joined = lax.psum(table_slots, ("dp", "section"))
    shards = (
        lax.psum_scatter(a_gain, "dp", scatter_dimension=0, tiled=True),
        lax.psum_scatter(a_shift, "dp", scatter_dimension=0, tiled=True),
        lax.psum_scatter(a_input, "dp", scatter_dimension=0, tiled=True),
        lax.psum_scatter(a_query, "dp", scatter_dimension=0, tiled=True),
        lax.psum_scatter(a_value, "dp", scatter_dimension=0, tiled=True),
        lax.psum_scatter(a_output, "dp", scatter_dimension=0, tiled=True),
        lax.psum_scatter(a_obias, "dp", scatter_dimension=0, tiled=True),
        lax.psum_scatter(a_scale, "dp", scatter_dimension=0, tiled=True),
        lax.psum_scatter(f_gain, "dp", scatter_dimension=0, tiled=True),
        lax.psum_scatter(f_shift, "dp", scatter_dimension=0, tiled=True),
        lax.psum_scatter(f_upward, "dp", scatter_dimension=0, tiled=True),
        lax.psum_scatter(f_ubias, "dp", scatter_dimension=0, tiled=True),
        lax.psum_scatter(f_downward, "dp", scatter_dimension=0, tiled=True),
        lax.psum_scatter(f_dbias, "dp", scatter_dimension=0, tiled=True),
        lax.psum_scatter(f_scale, "dp", scatter_dimension=0, tiled=True),
    )
    slotted = tuple((jnp.stack([piece * first_flag, piece * second_flag]) for piece in shards))
    joined = (
        lax.psum(slotted[0].astype(jnp.bfloat16), "section").astype(jnp.float32),
        lax.psum(slotted[1].astype(jnp.bfloat16), "section").astype(jnp.float32),
        lax.psum(slotted[2].astype(jnp.bfloat16), "section").astype(jnp.float32),
        lax.psum(slotted[3].astype(jnp.bfloat16), "section").astype(jnp.float32),
        lax.psum(slotted[4].astype(jnp.bfloat16), "section").astype(jnp.float32),
        lax.psum(slotted[5].astype(jnp.bfloat16), "section").astype(jnp.float32),
        lax.psum(slotted[6].astype(jnp.bfloat16), "section").astype(jnp.float32),
        lax.psum(slotted[7].astype(jnp.bfloat16), "section").astype(jnp.float32),
        lax.psum(slotted[8].astype(jnp.bfloat16), "section").astype(jnp.float32),
        lax.psum(slotted[9].astype(jnp.bfloat16), "section").astype(jnp.float32),
        lax.psum(slotted[10].astype(jnp.bfloat16), "section").astype(jnp.float32),
        lax.psum(slotted[11].astype(jnp.bfloat16), "section").astype(jnp.float32),
        lax.psum(slotted[12].astype(jnp.bfloat16), "section").astype(jnp.float32),
        lax.psum(slotted[13].astype(jnp.bfloat16), "section").astype(jnp.float32),
        lax.psum(slotted[14].astype(jnp.bfloat16), "section").astype(jnp.float32),
    )
    return (
        outputs[None],
        gradients[None],
        joined[0],
        joined[1],
        joined[2],
        joined[3],
        joined[4],
        table_joined,
        joined[5],
        joined[6],
        joined[7],
        joined[8],
        joined[9],
        joined[10],
        joined[11],
        joined[12],
        joined[13],
        joined[14],
    )


def solution(mesh):
    placed = (
        P("dp", None, None),
        P("dp", None, None),
        P("dp", None),
        P(),
        P(),
        P(),
        P(),
        P(),
        P(),
        P(),
        P(),
        P(),
        P(),
        P(),
        P(),
        P(),
        P(),
        P(),
        P(),
        P(),
    )
    return jax.shard_map(
        body,
        mesh=mesh,
        in_specs=placed,
        out_specs=(
            P("section", "dp", None, None),
            P("section", "dp", None, None),
            P(None, "dp"),
            P(None, "dp"),
            P(None, "dp", None),
            P(None, "dp"),
            P(None, "dp"),
            P(),
            P(None, "dp", None),
            P(None, "dp"),
            P(None, "dp"),
            P(None, "dp"),
            P(None, "dp"),
            P(None, "dp", None),
            P(None, "dp"),
            P(None, "dp", None),
            P(None, "dp"),
            P(None, "dp"),
        ),
        check_vma=False,
    )
```

profile of v0, /device:TPU:1, one launch (start us, length us, event | category | flops | bytes accessed | tf_op | source)
XLA Modules:
  0.0 1083.6 jit_solution(3358368168336070399)
XLA Ops:
  26.9 8.6 reshape.1046
  46.4 20.5 %rev.6 = f32[12,256,256]{2,1,0:T(8,128)S(1)} reverse(f32[12,256,256]{2,1,0:T(8,128)} %slice.168), dimensions={1} | reverse | bytes 6291456 | tf_op jit(solution)/shard_map/rev | solution.py:50
  72.4 29.8 %conditional.100 = (bf16[256,768]{1,0:T(8,128)(2,1)}, f32[256,768]{1,0:T(8,128)}) conditional(s32[]{:T(128)} %convert_element_type.1156, () %tuple.318, (s32[]{:T(128)}, bf16[1,256,768]{2,1,0:T(8,128)(2,1)}, pred[256,768]{1,0:T(8,128)(4,1)}, bf16[256,768]{1,0:T(8,128)(2,1)}, f32[768]{0:T(1024)S(1)}, /*index=5*/f32[768]{0:T(1024)S(1)}, ...), branch_computations={%region_0.1_spmd, %region_1.10_spmd} | conditional | flops 2427322624 | bytes 50346280 | solution.py:302
  73.7 28.2 %conditional.130 = (f32[256,768]{1,0:T(8,128)}, bf16[256,768]{1,0:T(8,128)(2,1)}) conditional(s32[]{:T(128)} %convert_element_type.887, (bf16[256,768]{1,0:T(8,128)(2,1)S(1)}, f32[768]{0:T(1024)S(1)}, f32[768]{0:T(1024)S(1)}, bf16[768,3072]{1,0:T(8,128)(2,1)}, f32[3072]{0:T(1024)}, /*index=5*/bf16[3072,768]{1,0:T(8,128)(2,1)}, f32[768]{0:T(1024)}, ...), branch_computations={%region_2.4_spmd, %region_5.9_spmd} | conditional | flops 2427126016 | bytes 48969832
  112.2 28.0 %conditional.101 = (bf16[256,768]{1,0:T(8,128)(2,1)}, f32[256,768]{1,0:T(8,128)}) conditional(s32[]{:T(128)} %convert_element_type.1157, () %tuple.320, (s32[]{:T(128)}, bf16[256,768]{1,0:T(8,128)(2,1)S(1)}, f32[768]{0:T(1024)S(1)}, f32[768]{0:T(1024)S(1)}, bf16[768,3072]{1,0:T(8,128)(2,1)}, /*index=5*/f32[3072]{0:T(1024)}, ...), branch_computations={%region_10.11_spmd, %region_11.20_spmd} | conditional | flops 2427126016 | bytes 48970024 | solution.py:302
  112.2 28.0 %conditional.131 = (f32[256,768]{1,0:T(8,128)}, bf16[256,768]{1,0:T(8,128)(2,1)}) conditional(s32[]{:T(128)} %convert_element_type.901, (bf16[256,768]{1,0:T(8,128)(2,1)S(1)}, f32[768]{0:T(1024)S(1)}, f32[768]{0:T(1024)S(1)}, bf16[768,3072]{1,0:T(8,128)(2,1)}, f32[3072]{0:T(1024)}, /*index=5*/bf16[3072,768]{1,0:T(8,128)(2,1)}, f32[768]{0:T(1024)}, ...), branch_computations={%region_12.14_spmd, %region_15.19_spmd} | conditional | flops 2427126016 | bytes 48969832
  149.6 8.6 conditional.102
  192.1 30.0 %conditional.105 = (bf16[256,768]{1,0:T(8,128)(2,1)}, f32[768]{0:T(1024)}, f32[768]{0:T(1024)}, f32[768,2304]{1,0:T(8,128)}, f32[768]{0:T(1024)}, /*index=5*/f32...) conditional(s32[]{:T(128)} %convert_element_type.1161, ...), branch_computations={%region_50.51_spmd, %region_51.76_spmd} | conditional | flops 6075181056 | bytes 150268096 | solution.py:352
  223.4 34.3 %collective-permute-done.4 = bf16[256,768]{1,0:T(8,128)(2,1)S(1)} collective-permute-done((bf16[256,768]{1,0:T(8,128)(2,1)}, bf16[256,768]{1,0:T(8,128)(2,1)S(1)}, u32[]{:S(2)}, u32[]{:S(2)}) %collective-permute-start.4) | collective-permute-done | bytes 393248 | tf_op jit(solution)/shard_map/ppermute | solution.py:13
  266.5 7.9 collective-permute-done.5
  274.4 7.7 conditional.107
  283.3 131.4 %collective-permute-done.6 = bf16[256,768]{1,0:T(8,128)(2,1)S(1)} collective-permute-done((bf16[256,768]{1,0:T(8,128)(2,1)}, bf16[256,768]{1,0:T(8,128)(2,1)S(1)}, u32[]{:S(2)}, u32[]{:S(2)}) %collective-permute-start.6) | collective-permute-done | bytes 393248 | tf_op jit(solution)/shard_map/ppermute | solution.py:13
  414.8 69.7 %conditional.108 = (bf16[256,768]{1,0:T(8,128)(2,1)}, f32[768]{0:T(1024)}, f32[768]{0:T(1024)}, f32[768,2304]{1,0:T(8,128)}, f32[768]{0:T(1024)}, /*index=5*/f32...) conditional(s32[]{:T(128)} %convert_element_type.1164, ...), branch_computations={%region_128.129_spmd, %region_129.154_spmd} | conditional | flops 6079906816 | bytes 147165728 | solution.py:352
  419.9 64.2 %conditional.138 = (f32[768]{0:T(1024)}, f32[768]{0:T(1024)}, f32[768,2304]{1,0:T(8,128)}, f32[768]{0:T(1024)}, f32[768]{0:T(1024)}, /*index=5*/f32[768,768]{1,0...) conditional(s32[]{:T(128)} %convert_element_type.1091, ...), branch_computations={%region_130.139_spmd, %region_140.153_spmd} | conditional | flops 6079710208 | bytes 137056032
  493.3 63.0 %conditional.109 = (bf16[256,768]{1,0:T(8,128)(2,1)}, f32[768]{0:T(1024)}, f32[768]{0:T(1024)}, f32[768,2304]{1,0:T(8,128)}, f32[768]{0:T(1024)}, /*index=5*/f32...) conditional(s32[]{:T(128)} %convert_element_type.1165, ...), branch_computations={%region_154.155_spmd, %region_155.180_spmd} | conditional | flops 6079906816 | bytes 118841720 | solution.py:352
  498.4 57.7 %conditional.139 = (f32[768]{0:T(1024)}, f32[768]{0:T(1024)}, f32[768,2304]{1,0:T(8,128)}, f32[768]{0:T(1024)}, f32[768]{0:T(1024)}, /*index=5*/f32[768,768]{1,0...) conditional(s32[]{:T(128)} %convert_element_type.1128, ...), branch_computations={%region_156.165_spmd, %region_166.179_spmd} | conditional | flops 6079710208 | bytes 108732032
  565.8 131.8 %all-reduce.13 = (f32[768]{0:T(1024)S(1)}, f32[768]{0:T(1024)S(1)}, f32[768]{0:T(1024)S(1)}, f32[768]{0:T(1024)S(1)}, f32[768]{0:T(1024)S(1)}, /*index=5*/f32[76...) all-reduce(f32[768]{0:T(1024)} %get-tuple-element.4176, ...), channel_id=2, replica_groups=mesh['dp'=32,'section'=4] {'dp'}, use_global_device_ids=true, to_apply=%region_180.181.clone | all-reduce | flops 10752 | bytes 86016
  700.0 36.8 %reduce-scatter.5.cloned.1.call-done = f32[24,2304]{1,0:T(8,128)} async-done(((f32[768,2304]{1,0:T(8,128)}), f32[24,2304]{1,0:T(8,128)}) %reduce-scatter.5.cloned.1.call-update) | async-done | bytes 221200 | tf_op jit(solution)/shard_map/reduce_scatter | solution.py:375
  738.5 97.4 %reduce-scatter.9.cloned.1.call-done = f32[24,3072]{1,0:T(8,128)} async-done(((f32[768,3072]{1,0:T(8,128)}), f32[24,3072]{1,0:T(8,128)}) %reduce-scatter.9.cloned.1.call-update) | async-done | bytes 294928 | tf_op jit(solution)/shard_map/reduce_scatter | solution.py:383
  837.6 96.7 %reduce-scatter.11.cloned.1.call-done = f32[96,768]{1,0:T(8,128)} async-done(((f32[3072,768]{1,0:T(8,128)}), f32[96,768]{1,0:T(8,128)}) %reduce-scatter.11.cloned.1.call-update) | async-done | bytes 294928 | tf_op jit(solution)/shard_map/reduce_scatter | solution.py:385
  936.3 8.6 all-reduce.14
  951.0 22.4 %rev.7 = f32[12,256,256]{1,2,0:T(8,128)S(1)} reverse(f32[12,256,256]{1,2,0:T(8,128)} %get-tuple-element.4181), dimensions={1} | reverse | bytes 6291456 | tf_op jit(solution)/shard_map/rev | solution.py:56
  988.1 9.3 reshape.1049
  1001.2 66.1 %psum.117 = f32[2,12,32]{2,1,0:T(8,128)S(1)} all-reduce(f32[2,12,32]{2,1,0:T(8,128)S(1)} %pad_maximum_fusion.19), channel_id=1, replica_groups=mesh['dp'=32,'section'=4] {'dp','section'}, use_global_device_ids=true, to_apply=%region_191.192 | all-reduce | flops 768 | bytes 6144 | tf_op jit(solution)/shard_map/psum | solution.py:371
  (464 shorter events, 377.0 us)
Async XLA Ops:
  7.2 691.2 %reduce-scatter.7.cloned.1.call-start = ((), (), s32[]{:S(2)}) async-start(), calls=%async_computation.5 | async-start | bytes 2433024 | tf_op jit(solution)/shard_map/reduce_scatter | solution.py:378
  46.3 20.7 %copy-start.177 = (f32[2,768]{1,0:T(2,128)S(1)}, f32[2,768]{1,0:T(2,128)}, u32[]{:S(2)}) copy-start(f32[2,768]{1,0:T(2,128)} %param.68) | copy-start | bytes 18436
  46.3 20.7 %copy-start.178 = (f32[2,768]{1,0:T(2,128)S(1)}, f32[2,768]{1,0:T(2,128)}, u32[]{:S(2)}) copy-start(f32[2,768]{1,0:T(2,128)} %param.67) | copy-start | bytes 18436
  46.3 21.3 %copy-start.179 = (f32[2,768]{1,0:T(2,128)S(1)}, f32[2,768]{1,0:T(2,128)}, u32[]{:S(2)}) copy-start(f32[2,768]{1,0:T(2,128)} %param.71) | copy-start | bytes 18436
  46.4 21.3 %copy-start.180 = (f32[2,768]{1,0:T(2,128)S(1)}, f32[2,768]{1,0:T(2,128)}, u32[]{:S(2)}) copy-start(f32[2,768]{1,0:T(2,128)} %param.72) | copy-start | bytes 18436
  46.4 21.9 %copy-start.181 = (f32[2,768]{1,0:T(2,128)S(1)}, f32[2,768]{1,0:T(2,128)}, u32[]{:S(2)}) copy-start(f32[2,768]{1,0:T(2,128)} %param.73) | copy-start | bytes 18436
  46.4 21.9 %copy-start.182 = (f32[2,768]{1,0:T(2,128)S(1)}, f32[2,768]{1,0:T(2,128)}, u32[]{:S(2)}) copy-start(f32[2,768]{1,0:T(2,128)} %param.74) | copy-start | bytes 18436
  46.4 21.9 %copy-start.183 = (f32[2,768]{1,0:T(2,128)S(1)}, f32[2,768]{1,0:T(2,128)}, u32[]{:S(2)}) copy-start(f32[2,768]{1,0:T(2,128)} %param.78) | copy-start | bytes 18436
  46.4 21.9 %copy-start.184 = (f32[2,768]{1,0:T(2,128)S(1)}, f32[2,768]{1,0:T(2,128)}, u32[]{:S(2)}) copy-start(f32[2,768]{1,0:T(2,128)} %param.79) | copy-start | bytes 18436
  102.3 8.9 collective-permute-start
  140.2 8.3 collective-permute-start.1
  158.2 11.3 %collective-permute-start.2 = (bf16[256,768]{1,0:T(8,128)(2,1)}, bf16[256,768]{1,0:T(8,128)(2,1)S(1)}, u32[]{:S(2)}, u32[]{:S(2)}) collective-permute-start(bf16[256,768]{1,0:T(8,128)(2,1)} %get-tuple-element.4099), channel_id=1, source_target_pairs={{0,1},{1,2},{2,3},{4,5},{5,6},{6,7},{8,9},{9,10},{10,11},{12,13},{... | collective-permute-start | bytes 1179656 | tf_op jit(solution)/shard_map/ppermute | solution.py:13
  172.3 11.2 %collective-permute-start.3 = (bf16[256,768]{1,0:T(8,128)(2,1)}, bf16[256,768]{1,0:T(8,128)(2,1)S(1)}, u32[]{:S(2)}, u32[]{:S(2)}) collective-permute-start(bf16[256,768]{1,0:T(8,128)(2,1)} %get-tuple-element.4100), channel_id=1, source_target_pairs={{0,1},{1,2},{2,3},{4,5},{5,6},{6,7},{8,9},{9,10},{10,11},{12,13},{... | collective-permute-start | bytes 1179656 | tf_op jit(solution)/shard_map/ppermute | solution.py:13
  222.1 35.6 %collective-permute-start.4 = (bf16[256,768]{1,0:T(8,128)(2,1)}, bf16[256,768]{1,0:T(8,128)(2,1)S(1)}, u32[]{:S(2)}, u32[]{:S(2)}) collective-permute-start(bf16[256,768]{1,0:T(8,128)(2,1)} %get-tuple-element.4107), channel_id=1, source_target_pairs={{1,0},{2,1},{3,2},{5,4},{6,5},{7,6},{9,8},{10,9},{11,10},{13,12},{... | collective-permute-start | bytes 1179656 | tf_op jit(solution)/shard_map/ppermute | solution.py:13
  265.2 9.2 collective-permute-start.5
  282.0 132.7 %collective-permute-start.6 = (bf16[256,768]{1,0:T(8,128)(2,1)}, bf16[256,768]{1,0:T(8,128)(2,1)S(1)}, u32[]{:S(2)}, u32[]{:S(2)}) collective-permute-start(bf16[256,768]{1,0:T(8,128)(2,1)} %get-tuple-element.4141), channel_id=1, source_target_pairs={{1,0},{2,1},{3,2},{5,4},{6,5},{7,6},{9,8},{10,9},{11,10},{13,12},{... | collective-permute-start | bytes 1179656 | tf_op jit(solution)/shard_map/ppermute | solution.py:13
  484.5 8.8 collective-permute-start.7
  556.4 180.4 %reduce-scatter.5.cloned.1.call-start = ((), (), s32[]{:S(2)}) async-start(), calls=%async_computation.4 | async-start | bytes 7299072 | tf_op jit(solution)/shard_map/reduce_scatter | solution.py:375
  557.1 278.8 %reduce-scatter.9.cloned.1.call-start = ((), (), s32[]{:S(2)}) async-start(), calls=%async_computation.6 | async-start | bytes 9732096 | tf_op jit(solution)/shard_map/reduce_scatter | solution.py:383
  557.9 376.5 %reduce-scatter.11.cloned.1.call-start = ((), (), s32[]{:S(2)}) async-start(), calls=%async_computation.7 | async-start | bytes 9732096 | tf_op jit(solution)/shard_map/reduce_scatter | solution.py:385
  558.4 511.3 %all-reduce.18.cloned.1.call-start = ((), (), s32[]{:S(2)}) async-start(), calls=%async_computation.8 | async-start | bytes 1769472 | tf_op jit(solution)/shard_map/psum | solution.py:393
  564.8 386.2 %copy-start.30 = (bf16[2,256,768]{2,1,0:T(8,128)(2,1)}, bf16[2,256,768]{2,1,0:T(8,128)(2,1)S(1)}, u32[]{:S(2)}) copy-start(bf16[2,256,768]{2,1,0:T(8,128)(2,1)S(1)} %bitcast_dynamic-update-slice_fusion.6) | copy-start | bytes 2359300
  997.4 70.5 %copy-start.31 = (bf16[2,256,768]{2,1,0:T(8,128)(2,1)S(1)}, bf16[2,256,768]{2,1,0:T(8,128)(2,1)}, u32[]{:S(2)}) copy-start(bf16[2,256,768]{2,1,0:T(8,128)(2,1)} %copy-done.30) | copy-start | bytes 2359300
  997.4 79.3 %copy-start.1 = (bf16[2,768,768]{2,1,0:T(8,128)(2,1)S(1)}, bf16[2,768,768]{2,1,0:T(8,128)(2,1)}, u32[]{:S(2)}) copy-start(bf16[2,768,768]{2,1,0:T(8,128)(2,1)} %param.70) | copy-start | bytes 7077892
  (80 other events, 362.9 us)
Sparse Core Ops, SparseCore 0:
  556.5 88.8 reduce-scatter.6
  649.7 87.0 reduce-scatter.4
  741.0 94.8 reduce-scatter.8
  839.5 94.8 reduce-scatter.10
  938.1 44.4 all-reduce.17
where the time goes:
time: 1100 us; the launch traced here: 1080 us
  waiting for transfers between devices  418 us (38%)
  local copies, waits for them, and re-layouts  217 us (20%)
  blocking collectives  206 us (19%)
  other arithmetic  88.2 us (8%)
  matrix products  85 us (8%)
  loops' own time  32.5 us (3%)
  starting transfers between devices  20.1 us (2%)
  between operations  16.3 us (1%)
    ppermute x8, waiting for transfers between devices, from_behind(): return lax.ppermute(shard, axis, pairs)  185 us
    unnamed x1, blocking collectives  132 us
    reduce_scatter x1, waiting for transfers between devices, body(): lax.psum_scatter(f_upward, 'dp', scatter_dimension=0, tiled=True)  97.4 us
    reduce_scatter x1, waiting for transfers between devices, body(): lax.psum_scatter(f_downward, 'dp', scatter_dimension=0, tiled=True)  96.7 us
    psum x1, blocking collectives, body(): table_joined = lax.psum(table_slots, ('dp', 'section'))  66.1 us
    reduce_scatter x1, waiting for transfers between devices, body(): lax.psum_scatter(a_input, 'dp', scatter_dimension=0, tiled=True)  36.8 us
    unnamed x166, local copies, waits for them, and re-layouts  28.7 us
    rev x1, local copies, waits for them, and re-layouts, fold_offsets(): flipped = grad_scores[:, ::-1, :]  22.4 us
  transfers between devices with their start and end apart: 13, of which 10 were waited for; matrix products, arithmetic and copies ran while one was open for 8% of the time, Pallas kernels for 0%

commit v1 on v0

v1 whole, which is shorter than its diff:
```python
import functools
import jax
import jax.numpy as jnp
from jax import lax
from jax.experimental import pallas as pl
from jax.experimental.pallas import tpu as pltpu
from jax.sharding import PartitionSpec as P

D, H, HD, FF, NB, MB = 768, 12, 64, 3072, 32, 256
R = 512
EPS = 1e-5
UF, UP, UL = 6, 6, 8
F32, BF16 = jnp.float32, jnp.bfloat16
C0 = 0.7978845608028654
C1 = 0.044715 * C0


def dot(a, b):
    return jnp.dot(a, b, preferred_element_type=F32)


def dot_rt(a, b):
    return lax.dot_general(a, b, (((1,), (1,)), ((), ())), preferred_element_type=F32)


def dot_lt(a, b):
    return lax.dot_general(a, b, (((0,), (0,)), ((), ())), preferred_element_type=F32)


def fold8(v):
    return jnp.sum(v.reshape(v.shape[0] // 8, 8, v.shape[1]), axis=0)


def rowsum(v):
    return jnp.sum(v, axis=0, keepdims=True)


def k1(yfun, tok, cot, pages, bucket, ag, ash, win, qb, vb, tab, wout, ob, asc, fg, fsh, wup, ub, wdn, db, fsc,
       so, go, parts, vec, e_st, af_st, dg_st,
       xs, low, qkv, E, mixed, br, af, dg, w_in, w_out, w_up, w_dn, T, cotv, gb, gm, glow, AB, vsc, Dsc, fch, ach,
       sem):
    y = yfun()
    def cp(src, dst, i):
        return pltpu.make_async_copy(src, dst, sem.at[i])
    def ldA(l):
        return [cp(win.at[l], w_in, 0), cp(wout.at[l], w_out, 1)]
    def ldF(l):
        return [cp(wup.at[l], w_up, 2), cp(wdn.at[l], w_dn, 3)]
    def start(cs):
        for c in cs: c.start()
    def wait(cs):
        for c in cs: c.wait()
    ctok = cp(tok, xs.at[0], 4)
    ccot = cp(cot, cotv, 5)
    ctok.start()
    start(ldA(0))
    start(ldF(0))
    ccot.start()
    lane = lax.broadcasted_iota(jnp.int32, (1, 128), 1)
    m0 = (lane < 64).astype(F32).astype(BF16)
    m1 = (lane >= 64).astype(F32).astype(BF16)
    lanef = lax.broadcasted_iota(jnp.int32, (MB, 128), 1).astype(F32)
    for mb in range(2):
        pf = jnp.broadcast_to(pages[mb:mb + 1, :].astype(F32), (128, MB)).T
        same = pf == lanef
        AB[0, mb] = jnp.where(same | (lanef > 7.5), 0.0, -1e30).astype(BF16)
        AB[1, mb] = jnp.where(same, 1.0, 0.0).astype(BF16)
    sel = (lax.broadcasted_iota(jnp.int32, (NB, 512), 0) == bucket[...]).astype(F32)

    def layernorm(s, gain, shift):
        def body(i, _):
            r = pl.ds(pl.multiple_of(i * 64, 64), 64)
            x = xs[s, r, :].astype(F32)
            c = x - jnp.mean(x, -1, keepdims=True)
            n = c * lax.rsqrt(jnp.mean(c * c, -1, keepdims=True) + EPS)
            low[s, r, :] = (n * gain + shift).astype(BF16)
            return 0
        lax.fori_loop(0, R // 64, body, 0, unroll=UL)

    def residual(s, val, bias, scale):
        b = val + bias
        br[s] = b.astype(BF16)
        xs[s + 1] = (xs[s].astype(F32) + scale * b).astype(BF16)

    def masks(g, mb, l):
        rows = pl.ds(pl.multiple_of(mb * MB, MB), MB)
        c = pl.multiple_of(g * 128, 128)
        q = qkv[l, rows, pl.ds(c, 128)]
        k = qkv[l, rows, pl.ds(D + c, 128)]
        v = qkv[l, rows, pl.ds(2 * D + c, 128)]
        km = jnp.concatenate([k * m0, k * m1], 0)
        vm = jnp.concatenate([v * m0, v * m1], 0)
        return rows, pl.ds(c, 128), q, km, vm

    def attn_fwd(l):
        s = 2 * l
        row = lambda ref: ref[pl.ds(l, 1), :]
        obias = lax.dot_general(tab[l], sel, (((1,), (0,)), ((), ())), precision=lax.Precision.HIGHEST, preferred_element_type=F32)
        def toep():
            base = [pltpu.roll(jnp.broadcast_to(obias[h:h + 1, :], (8, 512)), 257, 1, stride=1, stride_axis=0) for h in range(H)]
            base = jnp.concatenate(base, 0)
            for a in range(MB // 8):
                t = pltpu.roll(base, 8 * a, 1) if a else base
                for h in range(H):
                    T[h // 2, 8 * a:8 * a + 8, (h % 2) * MB:(h % 2) * MB + MB] = t[8 * h:8 * h + 8, :MB]
        with jax.named_scope('toep'):
            toep()
        layernorm(s, row(ag), row(ash))
        x = low[s]
        qkv[l, :, 0:D] = ((dot(x, w_in[:, 0:D]) + row(qb)) * 0.125).astype(BF16)
        qkv[l, :, D:2 * D] = dot(x, w_in[:, D:2 * D]).astype(BF16)
        qkv[l, :, 2 * D:3 * D] = (dot(x, w_in[:, 2 * D:3 * D]) + row(vb)).astype(BF16)
        def pair(it, _):
            mb, g = it // 6, it % 6
            rows, cols, q, km, vm = masks(g, mb, l)
            qx = jnp.concatenate([q, AB[0, mb]], 1)
            kx = jnp.concatenate([km, jnp.concatenate([AB[1, mb]] * 2, 0)], 1)
            sc = dot_rt(qx, kx) + T[g]
            s0, s1 = sc[:, :MB], sc[:, MB:]
            def soft(v):
                e = jnp.exp(v - jnp.max(v, -1, keepdims=True))
                return e * (1.0 / jnp.sum(e, -1, keepdims=True))
            e = jnp.concatenate([soft(s0), soft(s1)], 1).astype(BF16)
            E[it] = e
            mixed[l, rows, cols] = dot(e, vm).astype(BF16)
            return 0
        with jax.named_scope('pairs'):
            lax.fori_loop(0, 12, pair, 0, unroll=UP)
        residual(s, dot(mixed[l], w_out[...]), row(ob), row(asc))

    def ff_fwd(l):
        s = 2 * l + 1
        row = lambda ref: ref[pl.ds(l, 1), :]
        layernorm(s, row(fg), row(fsh))
        x = low[s]
        for j in range(4):
            u = dot(x, w_up[:, D * j:D * (j + 1)]) + ub[pl.ds(l, 1), D * j:D * (j + 1)]
            u2 = u * u
            t = jnp.tanh(u * (C0 + C1 * u2))
            h = 0.5 * t + 0.5
            af[:, D * j:D * (j + 1)] = (u * h).astype(BF16)
            dg[:, D * j:D * (j + 1)] = (h + (0.5 - 0.5 * t * t) * (u * (C0 + (3 * C1) * u2))).astype(BF16)
        residual(s, dot(af[...], w_dn[...]), row(db), row(fsc))

    def fwd(l, _):
        @pl.when(l == 1)
        def _():
            wait([cp(E, e_st, 6)])
        wait(ldA(l))
        attn_fwd(l)
        @pl.when(l == 0)
        def _():
            start(ldA(1))
            cp(E, e_st, 6).start()
        @pl.when(l == 1)
        def _():
            wait([cp(af, af_st, 7), cp(dg, dg_st, 8)])
        wait(ldF(l))
        ff_fwd(l)
        @pl.when(l == 0)
        def _():
            start(ldF(1))
            start([cp(af, af_st, 7), cp(dg, dg_st, 8)])
        return 0

    ctok.wait()
    lax.fori_loop(0, 2, fwd, 0)
    c_so = cp(xs.at[y + 1], so, 9)
    c_so.start()
    c_so.wait()
    ccot.wait()
    xs[4] = cotv[...]

    def head_back(s, scale):
        def body(i, c):
            a, b = c
            r = pl.ds(pl.multiple_of(i * 64, 64), 64)
            u = xs[s + 1, r, :].astype(F32)
            g = (u * scale).astype(BF16)
            gb[r, :] = g
            return a + fold8(u * br[s, r, :].astype(F32)), b + fold8(g.astype(F32))
        z = jnp.zeros((8, D), F32)
        a, b = lax.fori_loop(0, R // 64, body, (z, z), unroll=UL)
        return rowsum(a), rowsum(b)

    def tail_back(s, gain):
        def body(i, c):
            a, b = c
            r = pl.ds(pl.multiple_of(i * 64, 64), 64)
            x = xs[s, r, :].astype(F32)
            gl = glow[r, :]
            ce = x - jnp.mean(x, -1, keepdims=True)
            rs = lax.rsqrt(jnp.mean(ce * ce, -1, keepdims=True) + EPS)
            n = ce * rs
            gn = gl * n
            t = gl * gain
            u = xs[s + 1, r, :].astype(F32)
            o = u + rs * (t - jnp.mean(t, -1, keepdims=True) - n * jnp.mean(t * n, -1, keepdims=True))
            xs[s, r, :] = o.astype(BF16)
            return a + fold8(gn), b + fold8(gl)
        z = jnp.zeros((8, D), F32)
        a, b = lax.fori_loop(0, R // 64, body, (z, z), unroll=UL)
        return rowsum(a), rowsum(b)

    def put_rows(dst, b, val, nb):
        for o in range(16):
            zz, xx, cc = o // 8, (o // 2) % 4, o % 2
            rows = val[24 * o:24 * o + 24, :]
            chunk = jnp.concatenate([rows[:, 384 * k:384 * (k + 1)] for k in range(nb)], 0)
            dst[cc, 2 * b + zz, xx] = chunk.astype(BF16)

    def ff_bwd(l):
        s = 2 * l + 1
        row = lambda ref: ref[pl.ds(l, 1), :]
        v0 = l * 16
        sg, dbg = head_back(s, row(fsc))
        vsc[pl.ds(v0 + 9, 1), :] = sg
        vsc[pl.ds(v0 + 8, 1), :] = dbg
        g = gb[...]
        for j in range(4):
            c = slice(D * j, D * (j + 1))
            ga = dot_rt(g, w_dn[c, :])
            gbef = (ga * dg[:, c].astype(F32)).astype(BF16)
            dg[:, c] = gbef
            vsc[pl.ds(v0 + 10 + j, 1), :] = rowsum(fold8(gbef.astype(F32)))
        glow[...] = dot_rt(dg[...], w_up[...])
        @pl.when(y < 2)
        def _():
            def b2(b, _):
                a = low[s, :, pl.ds(pl.multiple_of(b * 384, 128), 384)]
                put_rows(fch, b, dot_lt(a, dg[:, pl.ds(pl.multiple_of(y * 1536, 128), 1536)]), 4)
                return 0
            lax.fori_loop(0, 2, b2, 0)
        @pl.when(y >= 2)
        def _():
            gq = gb[:, pl.ds(pl.multiple_of((y - 2) * 384, 128), 384)]
            def b4(zz, _):
                a = af[:, pl.ds(pl.multiple_of(zz * 768, 128), 768)]
                val = dot_lt(a, gq).astype(BF16)
                for o in range(8):
                    fch[o % 2, zz, o // 2] = val[96 * o:96 * o + 96, :]
                return 0
            lax.fori_loop(0, 4, b4, 0)
        gg, sh = tail_back(s, row(fg))
        vsc[pl.ds(v0 + 6, 1), :] = gg
        vsc[pl.ds(v0 + 7, 1), :] = sh
        c = cp(fch, parts.at[:, :, :, pl.ds(pl.multiple_of(96 * l, 96), 96), :], 9)
        c.start()
        c.wait()

    def attn_bwd(l):
        s = 2 * l
        row = lambda ref: ref[pl.ds(l, 1), :]
        v0 = l * 16
        sg, obg = head_back(s, row(asc))
        vsc[pl.ds(v0 + 5, 1), :] = sg
        vsc[pl.ds(v0 + 4, 1), :] = obg
        gm[...] = dot_rt(gb[...], w_out[...]).astype(BF16)
        def pair(it, _):
            mb, g = it // 6, it % 6
            rows, cols, q, km, vm = masks(g, mb, l)
            dop = gm[rows, cols]
            dp = dot_rt(dop, vm)
            e = E[it]
            ef = e.astype(F32)
            pt = ef * dp
            in0 = jnp.sum(pt[:, :MB], -1, keepdims=True) / jnp.sum(ef[:, :MB], -1, keepdims=True)
            in1 = jnp.sum(pt[:, MB:], -1, keepdims=True) / jnp.sum(ef[:, MB:], -1, keepdims=True)
            ds = jnp.concatenate([pt[:, :MB] - ef[:, :MB] * in0, pt[:, MB:] - ef[:, MB:] * in1], 1).astype(BF16)
            dsf = ds.astype(F32)
            @pl.when(mb == 0)
            def _():
                T[g] = dsf
            @pl.when(mb == 1)
            def _():
                T[g] = T[g] + dsf
            dv = dot_lt(e, dop)
            dk = dot_lt(ds, q)
            dq = dot(ds, km) * 0.125
            hm = lane < 64
            c0 = pl.multiple_of(g * 128, 128)
            qkv[l, rows, pl.ds(c0, 128)] = dq.astype(BF16)
            qkv[l, rows, pl.ds(D + c0, 128)] = jnp.where(hm, dk[:MB], dk[MB:]).astype(BF16)
            qkv[l, rows, pl.ds(2 * D + c0, 128)] = jnp.where(hm, dv[:MB], dv[MB:]).astype(BF16)
            return 0
        with jax.named_scope('pairs'):
            lax.fori_loop(0, 12, pair, 0, unroll=UP)
        def cs(i, c):
            a, b = c
            r = pl.ds(pl.multiple_of(i * 64, 64), 64)
            return a + fold8(qkv[l, r, 0:D].astype(F32)), b + fold8(qkv[l, r, 2 * D:3 * D].astype(F32))
        z = jnp.zeros((8, D), F32)
        a, b = lax.fori_loop(0, R // 64, cs, (z, z), unroll=UL)
        vsc[pl.ds(v0 + 2, 1), :] = rowsum(a)
        vsc[pl.ds(v0 + 3, 1), :] = rowsum(b)
        @pl.when(y < 3)
        def _():
            def b2(b, _):
                a = low[s, :, pl.ds(pl.multiple_of(b * 384, 128), 384)]
                put_rows(ach, b, dot_lt(a, qkv[l, :, pl.ds(pl.multiple_of(y * D, 128), D)]), 2)
                return 0
            lax.fori_loop(0, 2, b2, 0)
        @pl.when(y == 3)
        def _():
            def b2(b, _):
                a = mixed[l, :, pl.ds(pl.multiple_of(b * 384, 128), 384)]
                put_rows(ach, b, dot_lt(a, gb[...]), 2)
                return 0
            lax.fori_loop(0, 2, b2, 0)
        glow[...] = dot_rt(qkv[l], w_in[...])
        gg, sh = tail_back(s, row(ag))
        vsc[pl.ds(v0 + 0, 1), :] = gg
        vsc[pl.ds(v0 + 1, 1), :] = sh
        def fo(h, _):
            a = T[h // 2, :, pl.ds(pl.multiple_of((h % 2) * MB, MB), MB)]
            a = jnp.concatenate([a, jnp.zeros((MB, MB), F32)], 1)
            n = MB // 2
            while n >= 1:
                a = a[n:, :] + pltpu.roll(a[:n, :], n, 1)
                n //= 2
            Dsc[pl.ds(h, 1), :] = a
            return 0
        with jax.named_scope('fold'):
            lax.fori_loop(0, H, fo, 0, unroll=UF)
        tg = lax.dot_general(Dsc[...], sel, (((1,), (1,)), ((), ())), precision=lax.Precision.HIGHEST, preferred_element_type=F32)
        vsc[32:48, pl.ds(pl.multiple_of(l * 128, 128), 128)] = jnp.concatenate([tg, jnp.zeros((16, 96), F32)], 1)
        c = cp(ach, parts.at[:, :, :, pl.ds(pl.multiple_of(192 + 48 * l, 48), 48), :], 9)
        c.start()
        c.wait()

    vsc[...] = jnp.zeros_like(vsc)
    Dsc[...] = jnp.zeros_like(Dsc)

    def bwd(i, _):
        l = 1 - i
        @pl.when(l == 0)
        def _():
            wait(ldF(0))
            wait([cp(af_st, af, 7), cp(dg_st, dg, 8)])
        ff_bwd(l)
        @pl.when(l == 1)
        def _():
            start(ldF(0))
            start([cp(af_st, af, 7), cp(dg_st, dg, 8)])
        @pl.when(l == 0)
        def _():
            wait(ldA(0))
            wait([cp(e_st, E, 6)])
        attn_bwd(l)
        @pl.when(l == 1)
        def _():
            start(ldA(0))
            cp(e_st, E, 6).start()
        return 0
    lax.fori_loop(0, 2, bwd, 0)
    c_go = cp(xs.at[y], go, 9)
    c_go.start()
    c_v = cp(vsc, vec, 10)
    c_v.start()
    c_go.wait()
    c_v.wait()


def run_k1(yfun, tokens, cotangent, pages, bucket, ag, ash, win, qb, vb, tab, wout, ob, asc, fg, fsh, wup, ub, wdn, db, fsc):
    tok = tokens.reshape(R, D)
    cot = cotangent.reshape(R, D)
    bucket = jnp.pad(bucket, (0, 1), constant_values=-1).reshape(1, 512)
    ANY = pl.BlockSpec(memory_space=pl.ANY)
    V = pl.BlockSpec(memory_space=pltpu.VMEM)
    sds = jax.ShapeDtypeStruct
    outs = (sds((R, D), BF16), sds((R, D), BF16), sds((2, 4, 4, 288, 384), BF16), sds((48, D), F32),
            sds((12, MB, 512), BF16), sds((R, FF), BF16), sds((R, FF), BF16))
    vm = pltpu.VMEM
    scratch = [
        vm((5, R, D), BF16), vm((4, R, D), BF16), vm((2, R, 3 * D), BF16), vm((12, MB, 512), BF16),
        vm((2, R, D), BF16), vm((4, R, D), BF16), vm((R, FF), BF16), vm((R, FF), BF16),
        vm((D, 3 * D), BF16), vm((D, D), BF16), vm((D, FF), BF16), vm((FF, D), BF16),
        vm((6, MB, 512), F32), vm((R, D), BF16), vm((R, D), BF16), vm((R, D), BF16), vm((R, D), F32),
        vm((2, 2, MB, 128), BF16), vm((48, D), F32), vm((16, 512), F32), vm((2, 4, 4, 96, 384), BF16), vm((2, 4, 4, 48, 384), BF16),
        pltpu.SemaphoreType.DMA((11,)),
    ]
    return pl.pallas_call(
        functools.partial(k1, yfun),
        out_shape=outs,
        in_specs=[ANY, ANY, V, V, V, V, ANY, V, V, V, ANY, V, V, V, V, ANY, V, ANY, V, V],
        out_specs=(ANY,) * 7,
        scratch_shapes=scratch,
        compiler_params=pltpu.CompilerParams(vmem_limit_bytes=63400000),
        name="chain",
    )(tok, cot, pages, bucket, ag, ash, win, qb, vb, tab, wout, ob, asc, fg, fsh, wup, ub, wdn, db, fsc)


MESH = pl.DeviceIdType.MESH
UNITS = ((96, 96, 48), (240, 48, 32), (0, 96, 48), (192, 48, 16))


class Comm:
    def __init__(self, vec, s1, rc, rx1, rx2, s2, fin, G, vx, sems, semr, vsems, vsemr):
        d = lax.axis_index("dp")
        self.y = lax.axis_index("section")
        self.z, self.x, self.c = d // 8, (d // 2) % 4, d % 2
        self.vec, self.s1, self.rc, self.rx1, self.rx2, self.s2, self.fin, self.G, self.vx = vec, s1, rc, rx1, rx2, s2, fin, G, vx
        self.sems, self.semr, self.vsems, self.vsemr = sems, semr, vsems, vsemr

    def dev(self, z=None, x=None, c=None, y=None):
        z = self.z if z is None else z
        x = self.x if x is None else x
        c = self.c if c is None else c
        y = self.y if y is None else y
        return (z * 8 + x * 2 + c, y)

    def others(self, axis):
        me = getattr(self, axis)
        if axis == "c":
            return [1 - me]
        return [lax.rem(me + i, 4) for i in (2, 1, 3)]

    def barrier(self):
        b = pltpu.get_barrier_semaphore()
        for axis in "cxzy":
            for o in self.others(axis):
                pl.semaphore_signal(b, inc=1, device_id=self.dev(**{axis: o}), device_id_type=MESH)
        pl.semaphore_wait(b, 10)

    def copy(self, src, dst, s, r, device):
        return pltpu.make_async_remote_copy(src_ref=src, dst_ref=dst, send_sem=s, recv_sem=r, device_id=device, device_id_type=MESH)

    def halves(self, u):
        r0, n, a = UNITS[u]
        return (("x", "z", r0, a, 0), ("z", "x", r0 + a, n - a, 1))

    def c_copy(self, u, src):
        r0, n, _ = UNITS[u]
        o = 1 - self.c
        return self.copy(src, self.rc.at[:, :, r0:r0 + n, :], self.sems.at[u, 0, 0, 0], self.semr.at[u, 0, 0, 0], self.dev(c=o))

    def s1_src(self, axis, o, rows):
        return self.s1.at[:, o, rows, :] if axis == "x" else self.s1.at[o, :, rows, :]

    def s1_copy(self, u, half, o, slot):
        axis, _, r0, n, h = half
        rows = slice(r0, r0 + n)
        return self.copy(self.s1_src(axis, o, rows), self.rx1.at[slot, :, rows, :], self.sems.at[u, 1, h, o], self.semr.at[u, 1, h, slot],
                         self.dev(**{axis: o}))

    def s1_start(self, u, c_done):
        c_done()
        r0, n, _ = UNITS[u]

        def add(i, _):
            z, x = i // 4, i % 4
            self.s1[z, x, r0:r0 + n, :] = (self.s1[z, x, r0:r0 + n, :].astype(F32) + self.rc[z, x, r0:r0 + n, :].astype(F32)).astype(BF16)
            return 0
        lax.fori_loop(0, 16, add, 0)
        for half in self.halves(u):
            for o in self.others(half[0]):
                self.s1_copy(u, half, o, getattr(self, half[0])).start()

    def s2_copy(self, u, half, o, slot):
        _, axis, r0, n, h = half
        rows = slice(r0, r0 + n)
        return self.copy(self.s2.at[o, rows, :], self.rx2.at[slot, rows, :], self.sems.at[u, 2, h, o], self.semr.at[u, 2, h, slot],
                         self.dev(**{axis: o}))

    def s2_start(self, u):
        for half in self.halves(u):
            axis, axis2, r0, n, h = half
            me = getattr(self, axis)
            rows = slice(r0, r0 + n)
            for o in self.others(axis):
                self.s1_copy(u, half, o, o).wait_recv()

            def add(i, _):
                own = self.s1[i, me, rows, :] if axis == "x" else self.s1[me, i, rows, :]
                v = own.astype(F32)
                for o in self.others(axis):
                    v = v + self.rx1[o, i, rows, :].astype(F32)
                self.s2[i, rows, :] = v.astype(BF16)
                return 0
            lax.fori_loop(0, 4, add, 0)
            for o in self.others(axis2):
                self.s2_copy(u, half, o, getattr(self, axis2)).start()

    def y_copy(self, u, o, slot):
        r0, n, _ = UNITS[u]
        rows = slice(r0, r0 + n)
        return self.copy(self.fin.at[rows, :], self.G.at[slot, rows, :], self.sems.at[u, 3, 0, o], self.semr.at[u, 3, 0, slot], self.dev(y=o))

    def y_start(self, u):
        for half in self.halves(u):
            axis, axis2, r0, n, h = half
            me = getattr(self, axis2)
            rows = slice(r0, r0 + n)
            for o in self.others(axis2):
                self.s2_copy(u, half, o, o).wait_recv()
            v = self.s2[me, rows, :].astype(F32)
            for o in self.others(axis2):
                v = v + self.rx2[o, rows, :].astype(F32)
            v = v.astype(BF16)
            self.fin[rows, :] = v
            self.G[self.y, rows, :] = v
        for o in self.others("y"):
            self.y_copy(u, o, self.y).start()

    def y_done(self, u):
        for o in self.others("y"):
            self.y_copy(u, o, o).wait_recv()

    def sends_done(self, u, c_send):
        c_send()
        for half in self.halves(u):
            for o in self.others(half[0]):
                self.s1_copy(u, half, o, getattr(self, half[0])).wait_send()
            for o in self.others(half[1]):
                self.s2_copy(u, half, o, getattr(self, half[1])).wait_send()
        for o in self.others("y"):
            self.y_copy(u, o, self.y).wait_send()

    def v_copy(self, stage, axis, o, slot):
        return self.copy(self.vec, self.vx.at[stage, slot], self.vsems.at[stage, o], self.vsemr.at[stage, slot], self.dev(**{axis: o}))

    def v_start(self, stage):
        axis = "cxz"[stage]
        me = getattr(self, axis)
        for o in self.others(axis):
            self.v_copy(stage, axis, o, me).start()

    def v_finish(self, stage):
        axis = "cxz"[stage]
        me = getattr(self, axis)
        for o in self.others(axis):
            self.v_copy(stage, axis, o, o).wait_recv()
        for o in self.others(axis):
            self.v_copy(stage, axis, o, me).wait_send()
        self.vx[stage, me] = self.vec[...]
        v = self.vx[stage, 0] + self.vx[stage, 1]
        if stage:
            v = (v + self.vx[stage, 2]) + self.vx[stage, 3]
        self.vec[...] = v


def k2(parts, vec_in, G, vec, s1, rc, rx1, rx2, s2, fin, vx, lsem, sems, semr, vsems, vsemr):
    cm = Comm(vec, s1, rc, rx1, rx2, s2, fin, G, vx, sems, semr, vsems, vsemr)
    vec[...] = vec_in[...]
    locals_ = []
    for u, (r0, n, _) in enumerate(UNITS):
        locals_.append(pltpu.make_async_copy(parts.at[cm.c, :, :, r0:r0 + n, :], s1.at[:, :, r0:r0 + n, :], lsem.at[u]))
    for l in locals_:
        l.start()
    cm.barrier()
    csends = [cm.c_copy(u, parts.at[1 - cm.c, :, :, r0:r0 + n, :]) for u, (r0, n, _) in enumerate(UNITS)]
    cm.v_start(0)
    for c in csends:
        c.start()
    cm.v_finish(0)
    cm.v_start(1)
    for u in range(4):
        def c_done():
            locals_[u].wait()
            csends[u].wait_recv()
        cm.s1_start(u, c_done)
    cm.v_finish(1)
    cm.v_start(2)
    for u in range(4):
        cm.s2_start(u)
    for u in range(4):
        cm.y_start(u)
    cm.v_finish(2)
    for u in range(4):
        cm.y_done(u)
    for u in range(4):
        cm.sends_done(u, csends[u].wait_send)


def comm_scratch():
    vm = pltpu.VMEM
    return [vm((4, 4, 288, 384), BF16), vm((4, 4, 288, 384), BF16), vm((4, 4, 288, 384), BF16), vm((4, 288, 384), BF16),
            vm((4, 288, 384), BF16), vm((288, 384), BF16), vm((3, 4, 48, D), F32)]


def comm_sems():
    S = pltpu.SemaphoreType.DMA
    return [S((4, 4, 2, 4)), S((4, 4, 2, 4)), S((3, 4)), S((3, 4))]


def run_k2(parts, vec):
    V = pl.BlockSpec(memory_space=pltpu.VMEM)
    ANY = pl.BlockSpec(memory_space=pl.ANY)
    sds = jax.ShapeDtypeStruct
    return pl.pallas_call(
        k2,
        out_shape=(sds((4, 288, 384), BF16), sds((48, D), F32)),
        in_specs=[ANY, V],
        out_specs=(V, V),
        scratch_shapes=comm_scratch() + [pltpu.SemaphoreType.DMA((4,))] + comm_sems(),
        compiler_params=pltpu.CompilerParams(vmem_limit_bytes=48 << 20, collective_id=0, has_side_effects=True),
        name="reduce",
    )(parts, vec)


VEC_ROWS = (0, 1, 2, 3, 4, 5, 6, 7, 8, 9)


def k3(G, vec, a_gain, a_shift, w_in, qb, vb, tab, w_out, ob, asc, fg, fsh, w_up, ub, w_dn, db, fsc):
    d = lax.axis_index("dp")
    for l in range(2):
        for y in range(4):
            f = G[y, 96 * l:96 * l + 96, :].astype(F32)
            a = G[y, 192 + 48 * l:240 + 48 * l, :].astype(F32)
            if y < 2:
                for k in range(4):
                    w_up[l, :, 1536 * y + 384 * k:1536 * y + 384 * (k + 1)] = f[24 * k:24 * k + 24]
            else:
                w_dn[l, :, 384 * (y - 2):384 * (y - 1)] = f
            for k in range(2):
                if y < 3:
                    w_in[l, :, 768 * y + 384 * k:768 * y + 384 * (k + 1)] = a[24 * k:24 * k + 24]
                else:
                    w_out[l, :, 384 * k:384 * (k + 1)] = a[24 * k:24 * k + 24]
        r = pltpu.roll(vec[16 * l:16 * l + 16, :], lax.rem(D - 24 * d, D), 1)[:, :128]
        for ref, i in ((a_gain, 0), (a_shift, 1), (qb, 2), (vb, 3), (ob, 4), (asc, 5), (fg, 6), (fsh, 7), (db, 8), (fsc, 9)):
            ref[l:l + 1, :] = r[i:i + 1, :24]
        row = vec[pl.ds(16 * l + 10 + d // 8, 1), :]
        ub[l:l + 1, :] = pltpu.roll(jnp.broadcast_to(row, (8, D)), lax.rem(D - 96 * lax.rem(d, 8), D), 1)[0:1, :96]
        tab[l] = vec[32:32 + H, 128 * l:128 * l + NB]


def run_k3(G, vec):
    V = pl.BlockSpec(memory_space=pltpu.VMEM)
    sds = jax.ShapeDtypeStruct
    w = sds((2, 24), F32)
    outs = (w, w, sds((2, 24, 2304), F32), w, w, sds((2, H, NB), F32), sds((2, 24, D), F32), w, w, w, w, sds((2, 24, FF), F32), sds((2, 96), F32),
            sds((2, 96, D), F32), w, w)
    return pl.pallas_call(k3, out_shape=outs, in_specs=[V, V], out_specs=(V,) * 16, name="unpack",
                          compiler_params=pltpu.CompilerParams(vmem_limit_bytes=32 << 20))(G, vec)


def body(*args):
    so, go, parts, vec = run_k1(lambda: lax.axis_index("section"), *args)[:4]
    G, v = run_k2(parts, vec)
    return (so.reshape(1, 2, MB, D), go.reshape(1, 2, MB, D)) + tuple(run_k3(G, v))


def solution(mesh):
    data, whole = P("dp", None, None), P()
    w1, w2 = P(None, "dp"), P(None, "dp", None)
    return jax.shard_map(
        body,
        mesh=mesh,
        in_specs=(data, data, P("dp", None)) + (whole,) * 17,
        out_specs=(P("section", "dp", None, None),) * 2 + (w1, w1, w2, w1, w1, P(), w2, w1, w1, w1, w1, w2, w1, w2, w1, w1),
        check_vma=False,
    )
```

time: 1100 us -> 155 us (0.14); the launches traced: 1080 us -> 155 us
  waiting for transfers between devices: 418 us -> 0 us
  local copies, waits for them, and re-layouts: 217 us -> 4.09 us
  blocking collectives: 206 us -> 0 us
  Pallas kernels: 0 us -> 150 us
  other arithmetic: 88.2 us -> 0 us
  matrix products: 85 us -> 0 us
  loops' own time: 32.5 us -> 0 us
  starting transfers between devices: 20.1 us -> 0 us
  between operations: 16.3 us -> 0.68 us
    reduce_scatter x4 -> x0, waiting for transfers between devices: 231 us -> none  [the longest x1 97.4 us: body(): lax.psum_scatter(f_upward, 'dp', scatter_dimension=0, tiled=True)]
    ppermute x8 -> x0, waiting for transfers between devices: 185 us -> none  [from_behind(): return lax.ppermute(shard, axis, pairs)]
    pallas_call x0 -> x3, Pallas kernels: none -> 150 us  [the longest x1 91.8 us: run_k1(): pl.pallas_call(functools.partial(k1, yfun), out_shape=outs, in_specs=[ANY...]
    unnamed x1 -> x0, blocking collectives: 132 us -> none
    dot_general x32 -> x0, matrix products: 85 us -> none  [the longest x4 21.6 us: transposed_dot(): lax.dot_general(left, right, (((0,), (0,)), ((), ())), preferred_element_...]
    psum x2 -> x0, blocking collectives: 74.6 us -> none  [the longest x1 66.1 us: body(): table_joined = lax.psum(table_slots, ('dp', 'section'))]
    rev x2 -> x0, local copies, waits for them, and re-layouts: 42.9 us -> none  [the longest x1 22.4 us: fold_offsets(): flipped = grad_scores[:, ::-1, :]]
    another operation x10 -> x0, loops' own time: 31.3 us -> none  [the longest x5 21.1 us: body(): lax.cond(valid, run_backward, skip_backward, upstream, given, branch, pag...]
  transfers between devices with their start and end apart: 13 -> 0, of which waited for: 10 -> 0; matrix products, arithmetic and copies ran while one was open for 8% -> 0% of each run, Pallas kernels for 0% -> 0%
where the time goes in v1:
time: 155 us
  Pallas kernels  150 us (97%)
  local copies, waits for them, and re-layouts  4.09 us (3%)
    pallas_call x1, Pallas kernels, run_k1(): pl.pallas_call(functools.partial(k1, yfun), out_shape=outs, in_specs=[ANY...  91.8 us
    pallas_call x1, Pallas kernels, run_k2(): pl.pallas_call(k2, out_shape=(sds((4, 288, 384), BF16), sds((48, D), F32)...  56.9 us

profile of v1, /device:TPU:1, one launch (start us, length us, event | category | flops | bytes accessed | tf_op | source)
XLA Modules:
  0.0 154.8 jit_solution(13949597080900556416)
XLA Ops:
  0.7 1.3 pad.4
  1.9 1.3 copy.38.tab
  3.2 91.8 %chain.1 = (bf16[512,768]{1,0:T(8,128)(2,1)}, bf16[512,768]{1,0:T(8,128)(2,1)}, bf16[2,4,4,288,384]{4,3,2,1,0:T(8,128)(2,1)}, f32[48,768]{1,0:T(8,128)}, bf16[12...) custom-call(bf16[512,768]{1,0:T(8,128)(2,1)} %bitcast.5, bf16[512,768]{1,0:T(8,128)(2,1)} %bitcast.6, ...), custom_call_target="tpu_custom_call" | custom-call | tf_op jit(solution)/shard_map/chain/pallas_call | solution.py:382
  95.0 0.0 copy-start
  95.1 0.9 copy-done
  96.0 56.9 %reduce.1 = (bf16[4,288,384]{2,1,0:T(8,128)(2,1)S(1)}, f32[48,768]{1,0:T(8,128)S(1)}) custom-call(bf16[2,4,4,288,384]{4,3,2,1,0:T(8,128)(2,1)} %get-tuple-element.42.parts, f32[48,768]{1,0:T(8,128)S(1)} %copy-done), custom_call_target="tpu_custom_call" | custom-call | tf_op jit(solution)/shard_map/reduce/pallas_call | solution.py:590
  152.8 1.4 unpack.1
  154.2 0.6 copy.39
Async XLA Ops:
  95.0 0.9 copy-start

commit v2 on v1

v2 whole, which is shorter than its diff:
```python
import functools
import jax
import jax.numpy as jnp
from jax import lax
from jax.experimental import pallas as pl
from jax.experimental.pallas import tpu as pltpu
from jax.sharding import PartitionSpec as P

D, H, HD, FF, NB, MB = 768, 12, 64, 3072, 32, 256
R = 512
EPS = 1e-5
UF, UP, UL = 6, 6, 8
F32, BF16 = jnp.float32, jnp.bfloat16
C0 = 0.7978845608028654
C1 = 0.044715 * C0


def dot(a, b):
    return jnp.dot(a, b, preferred_element_type=F32)


def dot_rt(a, b):
    return lax.dot_general(a, b, (((1,), (1,)), ((), ())), preferred_element_type=F32)


def dot_lt(a, b):
    return lax.dot_general(a, b, (((0,), (0,)), ((), ())), preferred_element_type=F32)


def fold8(v):
    return jnp.sum(v.reshape(v.shape[0] // 8, 8, v.shape[1]), axis=0)


def rowsum(v):
    return jnp.sum(v, axis=0, keepdims=True)


MESH = pl.DeviceIdType.MESH
KINDS = ((96, 48, 0, 0), (48, 32, 192, 96))


class Comm:
    def __init__(self, vec, fch, ach, rc, rx1, rx2, s2, G, vx, sems, semr, vsems, vsemr, credit):
        d = lax.axis_index("dp")
        self.y = lax.axis_index("section")
        self.z, self.x, self.c = d // 8, lax.rem(d // 2, 4), lax.rem(d, 2)
        self.vec, self.own, self.rc, self.rx1, self.rx2, self.s2, self.G, self.vx = vec, (fch, ach), rc, rx1, rx2, s2, G, vx
        self.sems, self.semr, self.vsems, self.vsemr, self.credit = sems, semr, vsems, vsemr, credit

    def dev(self, axis, o):
        at = {"z": self.z, "x": self.x, "c": self.c, "y": self.y}
        at[axis] = o
        return (at["z"] * 8 + at["x"] * 2 + at["c"], at["y"])

    def others(self, axis):
        me = getattr(self, axis)
        if axis == "c":
            return [(1 - me, 0, 0)]
        return [(lax.rem(me + i, 4), 3 - i, i - 1) for i in (2, 1, 3)]

    def signal_all(self):
        b = pltpu.get_barrier_semaphore()
        for axis in "cxzy":
            for o, _, _ in self.others(axis):
                pl.semaphore_signal(b, inc=1, device_id=self.dev(axis, o), device_id_type=MESH)

    def wait_all(self):
        pl.semaphore_wait(pltpu.get_barrier_semaphore(), 10)

    def copy(self, src, dst, s, r, device):
        return pltpu.make_async_remote_copy(src_ref=src, dst_ref=dst, send_sem=s, recv_sem=r, device_id=device, device_id_type=MESH)

    def rows(self, kind, l, h=None):
        n, a, g, _ = KINDS[kind]
        base = g + n * l
        lo, m = (0, n) if h is None else ((0, a) if h == 0 else (a, n - a))
        return pl.ds(lo, m), pl.ds(pl.multiple_of(base + lo, 16), m)

    def unit(self, kind, l):
        return 2 * (1 - l) + kind

    def c_copy(self, kind, l):
        n, _, _, r = KINDS[kind]
        u = self.unit(kind, l)
        o = 1 - self.c
        return self.copy(self.own[kind].at[o], self.rc.at[:, :, r:r + n, :], self.sems.at[u, 0, 0, 0], self.semr.at[u, 0, 0, 0],
                         self.dev("c", o))

    def c_start(self, kind, l):
        if isinstance(l, int):
            if l == 0:
                pl.semaphore_wait(self.credit.at[kind], 1)
        else:
            @pl.when(l == 0)
            def _():
                pl.semaphore_wait(self.credit.at[kind], 1)
        self.c_copy(kind, l).start()

    def s1_copy(self, kind, l, h, o, there):
        axis = "xz"[h]
        u = self.unit(kind, l)
        mine, every = self.rows(kind, l, h)
        src = self.own[kind].at[self.c, :, o, mine, :] if axis == "x" else self.own[kind].at[self.c, o, :, mine, :]
        return self.copy(src, self.rx1.at[there, :, every, :], self.sems.at[u, 1, h, there], self.semr.at[u, 1, h, there], self.dev(axis, o))

    def s1_start(self, kind, l):
        n, _, _, r = KINDS[kind]
        own, c = self.own[kind], self.c
        cc = self.c_copy(kind, l)
        cc.wait_recv()

        def add(i, _):
            z, x = i // 4, lax.rem(i, 4)
            own[c, z, x] = (own[c, z, x].astype(F32) + self.rc[z, x, r:r + n, :].astype(F32)).astype(BF16)
            return 0
        lax.fori_loop(0, 16, add, 0)

        @pl.when(l == 1)
        def _():
            pl.semaphore_signal(self.credit.at[kind], inc=1, device_id=self.dev("c", 1 - c), device_id_type=MESH)
        for h in range(2):
            for o, there, _ in self.others("xz"[h]):
                self.s1_copy(kind, l, h, o, there).start()
        cc.wait_send()

    def s2_copy(self, kind, l, h, o, there):
        axis = "zx"[h]
        u = self.unit(kind, l)
        _, every = self.rows(kind, l, h)
        return self.copy(self.s2.at[o, every, :], self.rx2.at[there, every, :], self.sems.at[u, 2, h, there], self.semr.at[u, 2, h, there],
                         self.dev(axis, o))

    def s2_start(self, kind, l):
        own, c = self.own[kind], self.c
        for h in range(2):
            axis, axis2 = "xz"[h], "zx"[h]
            me = getattr(self, axis)
            mine, every = self.rows(kind, l, h)
            for o, _, here in self.others(axis):
                self.s1_copy(kind, l, h, o, here).wait_recv()

            def add(i, _):
                v = (own[c, i, me, mine, :] if axis == "x" else own[c, me, i, mine, :]).astype(F32)
                for k in range(3):
                    v = v + self.rx1[k, i, every, :].astype(F32)
                self.s2[i, every, :] = v.astype(BF16)
                return 0
            lax.fori_loop(0, 4, add, 0)
            for o, there, _ in self.others(axis2):
                self.s2_copy(kind, l, h, o, there).start()
            for o, there, _ in self.others(axis):
                self.s1_copy(kind, l, h, o, there).wait_send()

    def y_copy(self, kind, l, o, slot, there):
        u = self.unit(kind, l)
        _, every = self.rows(kind, l)
        part = self.G.at[slot, every, :]
        return self.copy(part, part, self.sems.at[u, 3, 0, there], self.semr.at[u, 3, 0, there], self.dev("y", o))

    def y_start(self, kind, l):
        for h in range(2):
            axis2 = "zx"[h]
            me = getattr(self, axis2)
            _, every = self.rows(kind, l, h)
            for o, _, here in self.others(axis2):
                self.s2_copy(kind, l, h, o, here).wait_recv()
            v = self.s2[me, every, :].astype(F32)
            for k in range(3):
                v = v + self.rx2[k, every, :].astype(F32)
            self.G[self.y, every, :] = v.astype(BF16)
            for o, there, _ in self.others(axis2):
                self.s2_copy(kind, l, h, o, there).wait_send()
        for o, there, _ in self.others("y"):
            self.y_copy(kind, l, o, self.y, there).start()

    def y_done(self, kind, l):
        for o, there, here in self.others("y"):
            self.y_copy(kind, l, o, o, here).wait_recv()
            self.y_copy(kind, l, o, self.y, there).wait_send()

    def v_copy(self, stage, o, there):
        i = (0, 1, 4)[stage] + there
        return self.copy(self.vec, self.vx.at[i], self.vsems.at[i], self.vsemr.at[i], self.dev("cxz"[stage], o))

    def v_start(self, stage):
        for o, there, _ in self.others("cxz"[stage]):
            self.v_copy(stage, o, there).start()

    def v_finish(self, stage):
        axis = "cxz"[stage]
        me = getattr(self, axis)
        for o, there, here in self.others(axis):
            self.v_copy(stage, o, here).wait_recv()
            self.v_copy(stage, o, there).wait_send()
        if stage == 0:
            self.vec[...] = self.vec[...] + self.vx[0]
            return
        own = self.vec[...]
        terms = []
        for p in range(4):
            slot = lax.rem(p - me + 7, 4)
            terms.append(jnp.where(slot == 3, own, self.vx[(1, 4)[stage - 1] + jnp.minimum(slot, 2)]))
        self.vec[...] = (terms[0] + terms[1]) + (terms[2] + terms[3])


def head_block(h):
    k = h % 6
    if isinstance(h, int):
        return h // 6, slice(MB * (k // 3), MB * (k // 3) + MB), slice(MB * (k % 3), MB * (k % 3) + MB)
    return h // 6, pl.ds(pl.multiple_of(MB * (k // 3), MB), MB), pl.ds(pl.multiple_of(MB * (k % 3), MB), MB)


def chain(tok, cot, pages, bucket, ag, ash, win, qb, vb, tab, wout, ob, asc, fg, fsh, wup, ub, wdn, db, fsc,
       so, go, G, vsc, e_st, af_st, dg_st,
       xs, low, qkv, E, mixed, br, af, dg, w_in, w_out, w_up, w_dn, T, AB, Dsc, bsc, fch, ach,
       rc, rx1, rx2, s2, vx, sem, sems, semr, vsems, vsemr, credit):
    cm = Comm(vsc, fch, ach, rc, rx1, rx2, s2, G, vx, sems, semr, vsems, vsemr, credit)
    y = cm.y
    def cp(src, dst, i):
        return pltpu.make_async_copy(src, dst, sem.at[i])
    def ldA(l):
        return [cp(win.at[l], w_in, 0), cp(wout.at[l], w_out, 1)]
    def ldF(l):
        return [cp(wup.at[l], w_up, 2), cp(wdn.at[l], w_dn, 3)]
    def start(cs):
        for c in cs: c.start()
    def wait(cs):
        for c in cs: c.wait()
    ctok = cp(tok, xs.at[0], 4)
    ccot = cp(cot, xs.at[5], 5)
    ctok.start()
    start(ldA(0))
    start(ldF(0))
    ccot.start()
    cm.signal_all()
    bsc[...] = jnp.full((1, 512), -1, jnp.int32)
    bsc[:, :511] = bucket[...]
    lane = lax.broadcasted_iota(jnp.int32, (1, 128), 1)
    m0 = (lane < 64).astype(F32).astype(BF16)
    m1 = (lane >= 64).astype(F32).astype(BF16)
    lanef = lax.broadcasted_iota(jnp.int32, (MB, 128), 1).astype(F32)
    for mb in range(2):
        pf = jnp.broadcast_to(pages[mb:mb + 1, :].astype(F32), (128, MB)).T
        same = pf == lanef
        AB[0, mb] = jnp.where(same | (lanef > 7.5), 0.0, -1e30).astype(BF16)
        AB[1, mb] = jnp.where(same, 1.0, 0.0).astype(BF16)
    sel = (lax.broadcasted_iota(jnp.int32, (NB, 512), 0) == bsc[...]).astype(F32)

    def layernorm(s, gain, shift):
        def body(i, _):
            r = pl.ds(pl.multiple_of(i * 64, 64), 64)
            x = xs[s, r, :].astype(F32)
            c = x - jnp.mean(x, -1, keepdims=True)
            n = c * lax.rsqrt(jnp.mean(c * c, -1, keepdims=True) + EPS)
            low[s, r, :] = (n * gain + shift).astype(BF16)
            return 0
        lax.fori_loop(0, R // 64, body, 0, unroll=UL)

    def residual(s, val, bias, scale):
        b = val + bias
        br[s] = b.astype(BF16)
        xs[s + 1] = (xs[s].astype(F32) + scale * b).astype(BF16)

    def masks(g, mb, l):
        rows = pl.ds(pl.multiple_of(mb * MB, MB), MB)
        c = pl.multiple_of(g * 128, 128)
        q = qkv[l, rows, pl.ds(c, 128)]
        k = qkv[l, rows, pl.ds(D + c, 128)]
        v = qkv[l, rows, pl.ds(2 * D + c, 128)]
        km = jnp.concatenate([k * m0, k * m1], 0)
        vm = jnp.concatenate([v * m0, v * m1], 0)
        return rows, pl.ds(c, 128), q, km, vm

    def attn_fwd(l):
        s = 2 * l
        row = lambda ref: ref[pl.ds(l, 1), :]
        obias = lax.dot_general(tab[:, pl.ds(l, 1), :].reshape(H, NB), sel, (((1,), (0,)), ((), ())), precision=lax.Precision.HIGHEST, preferred_element_type=F32)
        def toep():
            base = [pltpu.roll(jnp.broadcast_to(obias[h:h + 1, :], (8, 512)), 257, 1, stride=1, stride_axis=0) for h in range(H)]
            base = jnp.concatenate(base, 0)
            for a in range(MB // 8):
                t = pltpu.roll(base, 8 * a, 1) if a else base
                for h in range(H):
                    p, r, c = head_block(h)
                    T[p, r.start + 8 * a:r.start + 8 * a + 8, c] = t[8 * h:8 * h + 8, :MB]
        with jax.named_scope('toep'):
            toep()
        layernorm(s, row(ag), row(ash))
        x = low[s]
        qkv[l, :, 0:D] = ((dot(x, w_in[:, 0:D]) + row(qb)) * 0.125).astype(BF16)
        qkv[l, :, D:2 * D] = dot(x, w_in[:, D:2 * D]).astype(BF16)
        qkv[l, :, 2 * D:3 * D] = (dot(x, w_in[:, 2 * D:3 * D]) + row(vb)).astype(BF16)
        def pair(it, _):
            mb, g = it // 6, it % 6
            rows, cols, q, km, vm = masks(g, mb, l)
            qx = jnp.concatenate([q, AB[0, mb]], 1)
            kx = jnp.concatenate([km, jnp.concatenate([AB[1, mb]] * 2, 0)], 1)
            sc = dot_rt(qx, kx)
            s0, s1 = sc[:, :MB] + T[head_block(2 * g)], sc[:, MB:] + T[head_block(2 * g + 1)]
            def soft(v):
                e = jnp.exp(v - jnp.max(v, -1, keepdims=True))
                return e * (1.0 / jnp.sum(e, -1, keepdims=True))
            e = jnp.concatenate([soft(s0), soft(s1)], 1).astype(BF16)
            E[it] = e
            mixed[l, rows, cols] = dot(e, vm).astype(BF16)
            return 0
        with jax.named_scope('pairs'):
            lax.fori_loop(0, 12, pair, 0, unroll=UP)
        residual(s, dot(mixed[l], w_out[...]), row(ob), row(asc))

    def ff_fwd(l):
        s = 2 * l + 1
        row = lambda ref: ref[pl.ds(l, 1), :]
        layernorm(s, row(fg), row(fsh))
        x = low[s]
        for j in range(4):
            u = dot(x, w_up[:, D * j:D * (j + 1)]) + ub[pl.ds(l, 1), D * j:D * (j + 1)]
            u2 = u * u
            t = jnp.tanh(u * (C0 + C1 * u2))
            h = 0.5 * t + 0.5
            af[:, D * j:D * (j + 1)] = (u * h).astype(BF16)
            dg[:, D * j:D * (j + 1)] = (h + (0.5 - 0.5 * t * t) * (u * (C0 + (3 * C1) * u2))).astype(BF16)
        residual(s, dot(af[...], w_dn[...]), row(db), row(fsc))

    def fwd(l, _):
        @pl.when(l == 1)
        def _():
            wait([cp(E, e_st, 6)])
        wait(ldA(l))
        attn_fwd(l)
        @pl.when(l == 0)
        def _():
            start(ldA(1))
            cp(E, e_st, 6).start()
        @pl.when(l == 1)
        def _():
            wait([cp(af, af_st, 7), cp(dg, dg_st, 8)])
        wait(ldF(l))
        ff_fwd(l)
        @pl.when(l == 0)
        def _():
            start(ldF(1))
            start([cp(af, af_st, 7), cp(dg, dg_st, 8)])
        return 0

    ctok.wait()
    lax.fori_loop(0, 2, fwd, 0)
    c_so = cp(xs.at[y + 1], so, 9)
    c_so.start()
    ccot.wait()
    cm.wait_all()

    def up_slot(s):
        return jnp.where(s == 3, 5, s + 1)

    def head_back(s, scale):
        us = up_slot(s)

        def body(i, c):
            a, b = c
            r = pl.ds(pl.multiple_of(i * 64, 64), 64)
            u = xs[us, r, :].astype(F32)
            g = (u * scale).astype(BF16)
            b8 = fold8(u * br[s, r, :].astype(F32))
            br[s, r, :] = g
            return a + b8, b + fold8(g.astype(F32))
        z = jnp.zeros((8, D), F32)
        a, b = lax.fori_loop(0, R // 64, body, (z, z), unroll=UL)
        return rowsum(a), rowsum(b)

    def tail_back(s, gain):
        us = up_slot(s)

        def body(i, c):
            a, b = c
            r = pl.ds(pl.multiple_of(i * 64, 64), 64)
            x = xs[s, r, :].astype(F32)
            gl = T[0, r, :]
            ce = x - jnp.mean(x, -1, keepdims=True)
            rs = lax.rsqrt(jnp.mean(ce * ce, -1, keepdims=True) + EPS)
            n = ce * rs
            gn = gl * n
            t = gl * gain
            u = xs[us, r, :].astype(F32)
            o = u + rs * (t - jnp.mean(t, -1, keepdims=True) - n * jnp.mean(t * n, -1, keepdims=True))
            xs[s, r, :] = o.astype(BF16)
            return a + fold8(gn), b + fold8(gl)
        z = jnp.zeros((8, D), F32)
        a, b = lax.fori_loop(0, R // 64, body, (z, z), unroll=UL)
        @pl.when(y == s)
        def _():
            cp(xs.at[s], go, 10).start()
        return rowsum(a), rowsum(b)

    def put_rows(dst, b, val, nb):
        for o in range(16):
            zz, xx, cc = o // 8, (o // 2) % 4, o % 2
            rows = val[24 * o:24 * o + 24, :]
            chunk = jnp.concatenate([rows[:, 384 * k:384 * (k + 1)] for k in range(nb)], 0)
            dst[cc, 2 * b + zz, xx] = chunk.astype(BF16)

    def ff_bwd(l):
        s = 2 * l + 1
        row = lambda ref: ref[pl.ds(l, 1), :]
        v0 = l * 16
        sg, dbg = head_back(s, row(fsc))
        vsc[pl.ds(v0 + 9, 1), :] = sg
        vsc[pl.ds(v0 + 8, 1), :] = dbg
        @pl.when(l == 0)
        def _():
            cm.s1_start(1, 1)
            cm.y_start(0, 1)
        g = br[s]
        for j in range(4):
            c = slice(D * j, D * (j + 1))
            ga = dot_rt(g, w_dn[c, :])
            gbef = (ga * dg[:, c].astype(F32)).astype(BF16)
            dg[:, c] = gbef
            vsc[pl.ds(v0 + 10 + j, 1), :] = rowsum(fold8(gbef.astype(F32)))
        @pl.when(l == 0)
        def _():
            cm.s2_start(1, 1)
        @pl.when(y < 2)
        def _():
            def b2(b, _):
                a = low[s, :, pl.ds(pl.multiple_of(b * 384, 128), 384)]
                put_rows(fch, b, dot_lt(a, dg[:, pl.ds(pl.multiple_of(y * 1536, 128), 1536)]), 4)
                return 0
            lax.fori_loop(0, 2, b2, 0)
        @pl.when(y >= 2)
        def _():
            gq = br[s, :, pl.ds(pl.multiple_of((y - 2) * 384, 128), 384)]
            def b4(zz, _):
                a = af[:, pl.ds(pl.multiple_of(zz * 768, 128), 768)]
                val = dot_lt(a, gq).astype(BF16)
                for o in range(8):
                    fch[o % 2, zz, o // 2] = val[96 * o:96 * o + 96, :]
                return 0
            lax.fori_loop(0, 4, b4, 0)
        cm.c_start(0, l)
        T[0] = dot_rt(dg[...], w_up[...])
        @pl.when(l == 1)
        def _():
            c_so.wait()
        gg, sh = tail_back(s, row(fg))
        vsc[pl.ds(v0 + 6, 1), :] = gg
        vsc[pl.ds(v0 + 7, 1), :] = sh

    def attn_bwd(l):
        s = 2 * l
        row = lambda ref: ref[pl.ds(l, 1), :]
        v0 = l * 16
        sg, obg = head_back(s, row(asc))
        vsc[pl.ds(v0 + 5, 1), :] = sg
        vsc[pl.ds(v0 + 4, 1), :] = obg
        cm.s1_start(0, l)
        @pl.when(l == 0)
        def _():
            cm.y_start(1, 1)
        low[s + 1] = dot_rt(br[s], w_out[...]).astype(BF16)
        def pair(it, _):
            mb, g = it // 6, it % 6
            rows, cols, q, km, vm = masks(g, mb, l)
            dop = low[s + 1, rows, cols]
            dp = dot_rt(dop, vm)
            e = E[it]
            ef = e.astype(F32)
            pt = ef * dp
            in0 = jnp.sum(pt[:, :MB], -1, keepdims=True) / jnp.sum(ef[:, :MB], -1, keepdims=True)
            in1 = jnp.sum(pt[:, MB:], -1, keepdims=True) / jnp.sum(ef[:, MB:], -1, keepdims=True)
            ds = jnp.concatenate([pt[:, :MB] - ef[:, :MB] * in0, pt[:, MB:] - ef[:, MB:] * in1], 1).astype(BF16)
            dsf = ds.astype(F32)
            @pl.when(mb == 0)
            def _():
                T[head_block(2 * g)] = dsf[:, :MB]
                T[head_block(2 * g + 1)] = dsf[:, MB:]
            @pl.when(mb == 1)
            def _():
                for k in range(2):
                    b = head_block(2 * g + k)
                    T[b] = T[b] + dsf[:, MB * k:MB * k + MB]
            dv = dot_lt(e, dop)
            dk = dot_lt(ds, q)
            dq = dot(ds, km) * 0.125
            hm = lane < 64
            c0 = pl.multiple_of(g * 128, 128)
            qkv[l, rows, pl.ds(c0, 128)] = dq.astype(BF16)
            qkv[l, rows, pl.ds(D + c0, 128)] = jnp.where(hm, dk[:MB], dk[MB:]).astype(BF16)
            qkv[l, rows, pl.ds(2 * D + c0, 128)] = jnp.where(hm, dv[:MB], dv[MB:]).astype(BF16)
            return 0
        with jax.named_scope('pairs'):
            lax.fori_loop(0, 12, pair, 0, unroll=UP)
        cm.s2_start(0, l)
        def fo(h, _):
            a = T[head_block(h)]
            a = jnp.concatenate([a, jnp.zeros((MB, MB), F32)], 1)
            n = MB // 2
            while n >= 1:
                a = a[n:, :] + pltpu.roll(a[:n, :], n, 1)
                n //= 2
            Dsc[pl.ds(h, 1), :] = a
            return 0
        with jax.named_scope('fold'):
            lax.fori_loop(0, H, fo, 0, unroll=UF)
        tg = lax.dot_general(Dsc[...], sel, (((1,), (1,)), ((), ())), precision=lax.Precision.HIGHEST, preferred_element_type=F32)
        vsc[32:48, pl.ds(pl.multiple_of(l * 128, 128), 128)] = jnp.concatenate([tg, jnp.zeros((16, 96), F32)], 1)
        def cs(i, c):
            a, b = c
            r = pl.ds(pl.multiple_of(i * 64, 64), 64)
            return a + fold8(qkv[l, r, 0:D].astype(F32)), b + fold8(qkv[l, r, 2 * D:3 * D].astype(F32))
        z = jnp.zeros((8, D), F32)
        a, b = lax.fori_loop(0, R // 64, cs, (z, z), unroll=UL)
        vsc[pl.ds(v0 + 2, 1), :] = rowsum(a)
        vsc[pl.ds(v0 + 3, 1), :] = rowsum(b)
        @pl.when(y < 3)
        def _():
            def b2(b, _):
                a = low[s, :, pl.ds(pl.multiple_of(b * 384, 128), 384)]
                put_rows(ach, b, dot_lt(a, qkv[l, :, pl.ds(pl.multiple_of(y * D, 128), D)]), 2)
                return 0
            lax.fori_loop(0, 2, b2, 0)
        @pl.when(y == 3)
        def _():
            def b2(b, _):
                a = mixed[l, :, pl.ds(pl.multiple_of(b * 384, 128), 384)]
                put_rows(ach, b, dot_lt(a, br[s]), 2)
                return 0
            lax.fori_loop(0, 2, b2, 0)
        cm.c_start(1, l)
        T[0] = dot_rt(qkv[l], w_in[...])
        @pl.when(l == 0)
        def _():
            cm.s1_start(1, 0)
            cm.y_start(0, 0)
        gg, sh = tail_back(s, row(ag))
        vsc[pl.ds(v0 + 0, 1), :] = gg
        vsc[pl.ds(v0 + 1, 1), :] = sh

    vsc[...] = jnp.zeros_like(vsc)
    Dsc[...] = jnp.zeros_like(Dsc)

    def bwd(i, _):
        l = 1 - i
        @pl.when(l == 0)
        def _():
            wait(ldF(0))
            wait([cp(af_st, af, 7), cp(dg_st, dg, 8)])
        ff_bwd(l)
        @pl.when(l == 1)
        def _():
            start(ldF(0))
            start([cp(af_st, af, 7), cp(dg_st, dg, 8)])
        @pl.when(l == 0)
        def _():
            wait(ldA(0))
            wait([cp(e_st, E, 6)])
        attn_bwd(l)
        @pl.when(l == 1)
        def _():
            start(ldA(0))
            cp(e_st, E, 6).start()
        return 0
    lax.fori_loop(0, 2, bwd, 0)
    cm.v_start(0)
    cm.s2_start(1, 0)
    cm.v_finish(0)
    cm.v_start(1)
    cm.y_start(1, 0)
    cm.v_finish(1)
    cm.v_start(2)
    cp(xs.at[y], go, 10).wait()
    cm.v_finish(2)
    for l in range(2):
        for k in range(2):
            cm.y_done(k, l)


def run_chain(tokens, cotangent, pages, bucket, ag, ash, win, qb, vb, tab, wout, ob, asc, fg, fsh, wup, ub, wdn, db, fsc):
    tok = tokens.reshape(R, D)
    cot = cotangent.reshape(R, D)
    bucket = bucket.reshape(1, 511)
    tab = jnp.transpose(tab, (1, 0, 2))
    ANY = pl.BlockSpec(memory_space=pl.ANY)
    V = pl.BlockSpec(memory_space=pltpu.VMEM)
    sds = jax.ShapeDtypeStruct
    outs = (sds((R, D), BF16), sds((R, D), BF16), sds((4, 288, 384), BF16), sds((48, D), F32),
            sds((12, MB, 512), BF16), sds((R, FF), BF16), sds((R, FF), BF16))
    vm = pltpu.VMEM
    S = pltpu.SemaphoreType.DMA
    scratch = [
        vm((6, R, D), BF16), vm((4, R, D), BF16), vm((2, R, 3 * D), BF16), vm((12, MB, 512), BF16),
        vm((2, R, D), BF16), vm((4, R, D), BF16), vm((R, FF), BF16), vm((R, FF), BF16),
        vm((D, 3 * D), BF16), vm((D, D), BF16), vm((D, FF), BF16), vm((FF, D), BF16),
        vm((2, R, D), F32),
        vm((2, 2, MB, 128), BF16), vm((16, 512), F32), vm((1, 512), jnp.int32), vm((2, 4, 4, 96, 384), BF16), vm((2, 4, 4, 48, 384), BF16),
        vm((4, 4, 144, 384), BF16), vm((3, 4, 288, 384), BF16), vm((3, 288, 384), BF16), vm((4, 288, 384), BF16), vm((7, 48, D), F32),
        S((11,)), S((4, 4, 2, 4)), S((4, 4, 2, 4)), S((7,)), S((7,)), pltpu.SemaphoreType.REGULAR((2,)),
    ]
    return pl.pallas_call(
        chain,
        out_shape=outs,
        in_specs=[ANY, ANY, V, V, V, V, ANY, V, V, V, ANY, V, V, V, V, ANY, V, ANY, V, V],
        out_specs=(ANY, ANY, V, V, ANY, ANY, ANY),
        scratch_shapes=scratch,
        compiler_params=pltpu.CompilerParams(vmem_limit_bytes=63400000, collective_id=0, has_side_effects=True),
        name="chain",
    )(tok, cot, pages, bucket, ag, ash, win, qb, vb, tab, wout, ob, asc, fg, fsh, wup, ub, wdn, db, fsc)


def k3(G, vec, a_gain, a_shift, w_in, qb, vb, tab, w_out, ob, asc, fg, fsh, w_up, ub, w_dn, db, fsc):
    d = lax.axis_index("dp")
    for l in range(2):
        for y in range(4):
            f = G[y, 96 * l:96 * l + 96, :].astype(F32)
            a = G[y, 192 + 48 * l:240 + 48 * l, :].astype(F32)
            if y < 2:
                for k in range(4):
                    w_up[l, :, 1536 * y + 384 * k:1536 * y + 384 * (k + 1)] = f[24 * k:24 * k + 24]
            else:
                w_dn[l, :, 384 * (y - 2):384 * (y - 1)] = f
            for k in range(2):
                if y < 3:
                    w_in[l, :, 768 * y + 384 * k:768 * y + 384 * (k + 1)] = a[24 * k:24 * k + 24]
                else:
                    w_out[l, :, 384 * k:384 * (k + 1)] = a[24 * k:24 * k + 24]
        r = pltpu.roll(vec[16 * l:16 * l + 16, :], lax.rem(D - 24 * d, D), 1)[:, :128]
        for ref, i in ((a_gain, 0), (a_shift, 1), (qb, 2), (vb, 3), (ob, 4), (asc, 5), (fg, 6), (fsh, 7), (db, 8), (fsc, 9)):
            ref[l:l + 1, :] = r[i:i + 1, :24]
        row = vec[pl.ds(16 * l + 10 + d // 8, 1), :]
        ub[l:l + 1, :] = pltpu.roll(jnp.broadcast_to(row, (8, D)), lax.rem(D - 96 * lax.rem(d, 8), D), 1)[0:1, :96]
        tab[:, l, :] = vec[32:32 + H, 128 * l:128 * l + NB]


def run_k3(G, vec):
    V = pl.BlockSpec(memory_space=pltpu.VMEM)
    sds = jax.ShapeDtypeStruct
    w = sds((2, 24), F32)
    outs = (w, w, sds((2, 24, 2304), F32), w, w, sds((H, 2, NB), F32), sds((2, 24, D), F32), w, w, w, w, sds((2, 24, FF), F32), sds((2, 96), F32),
            sds((2, 96, D), F32), w, w)
    return pl.pallas_call(k3, out_shape=outs, in_specs=[V, V], out_specs=(V,) * 16, name="unpack",
                          compiler_params=pltpu.CompilerParams(vmem_limit_bytes=32 << 20))(G, vec)


def body(*args):
    so, go, G, v = run_chain(*args)[:4]
    outs = run_k3(G, v)
    return (so.reshape(1, 2, MB, D), go.reshape(1, 2, MB, D)) + tuple(outs[:5]) + (jnp.transpose(outs[5], (1, 0, 2)),) + tuple(outs[6:])


def solution(mesh):
    data, whole = P("dp", None, None), P()
    w1, w2 = P(None, "dp"), P(None, "dp", None)
    return jax.shard_map(
        body,
        mesh=mesh,
        in_specs=(data, data, P("dp", None)) + (whole,) * 17,
        out_specs=(P("section", "dp", None, None),) * 2 + (w1, w1, w2, w1, w1, P(), w2, w1, w1, w1, w1, w2, w1, w2, w1, w1),
        check_vma=False,
    )
```

time: 155 us -> 136 us (0.88)
  Pallas kernels: 150 us -> 129 us
    pallas_call x2 -> x1, Pallas kernels: 149 us -> 128 us  [run_chain(): pl.pallas_call(chain, out_shape=outs, in_specs=[ANY, ANY, V, V, V, V, ANY...]
    unnamed x4 -> x8, local copies, waits for them, and re-layouts: 2.82 us -> 5.02 us
where the time goes in v2:
time: 136 us; the launch traced here: 135 us
  Pallas kernels  129 us (95%)
  local copies, waits for them, and re-layouts  5.02 us (4%)
    pallas_call x1, Pallas kernels, run_chain(): pl.pallas_call(chain, out_shape=outs, in_specs=[ANY, ANY, V, V, V, V, ANY...  128 us
    unnamed x8, local copies, waits for them, and re-layouts  5.02 us

profile of v2, /device:TPU:1, one launch (start us, length us, event | category | flops | bytes accessed | tf_op | source)
XLA Modules:
  0.0 134.8 jit_solution(595861231640774548)
XLA Ops:
  0.7 127.8 %chain.1 = (bf16[512,768]{1,0:T(8,128)(2,1)}, bf16[512,768]{1,0:T(8,128)(2,1)}, bf16[4,288,384]{2,1,0:T(8,128)(2,1)}, f32[48,768]{1,0:T(8,128)}, bf16[12,256,512...) custom-call(bf16[512,768]{1,0:T(8,128)(2,1)} %bitcast.9, bf16[512,768]{1,0:T(8,128)(2,1)} %bitcast.10, ...), custom_call_target="tpu_custom_call" | custom-call | tf_op jit(solution)/shard_map/chain/pallas_call | solution.py:599
  128.5 0.0 copy-start
  128.5 1.2 copy-done
  129.6 0.0 copy-start.1
  129.6 0.9 copy-done.1
  130.5 0.0 copy-start.2
  130.5 1.3 unpack.1
  131.9 2.1 %copy.40 = bf16[1,2,256,768]{3,2,1,0:T(8,128)(2,1)} copy(bf16[1,2,256,768]{3,2,1,0:T(8,128)(2,1)} %bitcast.8) | data formatting | bytes 1572864
  133.9 0.0 copy-done.2
  133.9 0.9 copy.41
Async XLA Ops:
  128.5 1.2 copy-start
  129.6 0.9 copy-start.1
  130.5 3.4 %copy-start.2 = (bf16[512,768]{1,0:T(8,128)(2,1)S(1)}, bf16[512,768]{1,0:T(8,128)(2,1)}, u32[]{:S(2)}) copy-start(bf16[512,768]{1,0:T(8,128)(2,1)} %get-tuple-element.39) | copy-start | bytes 2359300

commit v3 on v2

v3 whole, which is shorter than its diff:
```python
import functools
import jax
import jax.numpy as jnp
from jax import lax
from jax.experimental import pallas as pl
from jax.experimental.pallas import tpu as pltpu
from jax.sharding import PartitionSpec as P

D, H, HD, FF, NB, MB = 768, 12, 64, 3072, 32, 256
R = 512
EPS = 1e-5
UP, UL = 12, 8
F32, BF16 = jnp.float32, jnp.bfloat16
C0 = 0.7978845608028654
C1 = 0.044715 * C0


def dot(a, b):
    return jnp.dot(a, b, preferred_element_type=F32)


def dot_rt(a, b):
    return lax.dot_general(a, b, (((1,), (1,)), ((), ())), preferred_element_type=F32)


def dot_lt(a, b):
    return lax.dot_general(a, b, (((0,), (0,)), ((), ())), preferred_element_type=F32)


def fold8(v):
    return jnp.sum(v.reshape(v.shape[0] // 8, 8, v.shape[1]), axis=0)


def rowsum(v):
    return jnp.sum(v, axis=0, keepdims=True)


MESH = pl.DeviceIdType.MESH
KINDS = ((96, 48, 0, 0), (48, 32, 192, 96))


class Comm:
    def __init__(self, vecs, fch, ach, rc, rx1, rx2, G, vxs, sems, semr, vsems, vsemr, credit):
        d = lax.axis_index("dp")
        self.y = lax.axis_index("section")
        self.z, self.x, self.c = d // 8, lax.rem(d // 2, 4), lax.rem(d, 2)
        self.vecs, self.own, self.rc, self.G, self.vxs = vecs, (fch, ach), rc, G, vxs
        self.rx1, self.rx2 = rx1, rx2
        self.sems, self.semr, self.vsems, self.vsemr, self.credit = sems, semr, vsems, vsemr, credit

    def dev(self, axis, o):
        at = {"z": self.z, "x": self.x, "c": self.c, "y": self.y}
        at[axis] = o
        return (at["z"] * 8 + at["x"] * 2 + at["c"], at["y"])

    def others(self, axis):
        me = getattr(self, axis)
        if axis == "c":
            return [(1 - me, 0, 0)]
        return [(lax.rem(me + i, 4), 3 - i, i - 1) for i in (2, 1, 3)]

    def signal_all(self):
        b = pltpu.get_barrier_semaphore()
        for axis in "cxzy":
            for o, _, _ in self.others(axis):
                pl.semaphore_signal(b, inc=1, device_id=self.dev(axis, o), device_id_type=MESH)

    def wait_all(self):
        pl.semaphore_wait(pltpu.get_barrier_semaphore(), 10)

    def copy(self, src, dst, sem, device):
        return pltpu.make_async_remote_copy(src_ref=src, dst_ref=dst, send_sem=self.sems.at[sem], recv_sem=self.semr.at[sem],
                                            device_id=device, device_id_type=MESH)

    def rows(self, kind, l, lo, m):
        n, _, g, _ = KINDS[kind]
        return pl.ds(lo, m), pl.ds(pl.multiple_of(g + n * l + lo, 16), m)

    def half(self, kind, h):
        n, a, _, _ = KINDS[kind]
        return (0, a) if h == 0 else (a, n - a)

    def unit(self, kind, l):
        return 2 * (1 - l) + kind

    def c_copy(self, kind, l):
        n, _, _, r = KINDS[kind]
        o = 1 - self.c
        return self.copy(self.own[kind].at[o], self.rc.at[:, :, r:r + n, :], (self.unit(kind, l), 0, 0), self.dev("c", o))

    def c_start(self, kind, l):
        @pl.when(l == 0)
        def _():
            pl.semaphore_wait(self.credit.at[kind], 1)
        self.c_copy(kind, l).start()

    def at(self, kind, axis, i, j, rows):
        own = self.own[kind]
        return own.at[self.c, j, i, rows, :] if axis == "x" else own.at[self.c, i, j, rows, :]

    def hops(self, kind, l, phase):
        out = []
        u = self.unit(kind, l)
        for h in range(2):
            axis, first = ("xz"[h], None) if phase == 1 else ("zx"[h], "xz"[h])
            me = getattr(self, axis)
            mine, every = self.rows(kind, l, *self.half(kind, h))
            j = pl.ds(0, 4) if phase == 1 else getattr(self, first)
            buf = self.rx1 if phase == 1 else self.rx2
            for o, there, here in self.others(axis):
                cps = []
                for slot in (there, here):
                    dst = buf.at[slot, :, every, :] if phase == 1 else buf.at[slot, every, :]
                    cps.append(self.copy(self.at(kind, axis, o, j, mine), dst, (u, phase, 3 * h + slot), self.dev(axis, o)))
                out.append((h, cps[0], cps[1]))
        return out

    def launch(self, kind, l, phase):
        for _, cp, _ in self.hops(kind, l, phase):
            cp.start()

    def land(self, kind, l, phase):
        hops = self.hops(kind, l, phase)
        for h in range(2):
            for hh, _, cp in hops:
                if hh == h:
                    cp.wait_recv()
            axis = "xz"[h] if phase == 1 else "zx"[h]
            me = getattr(self, axis)
            mine, every = self.rows(kind, l, *self.half(kind, h))

            def total(s, parts):
                v = s[...].astype(F32)
                for p in parts:
                    v = v + p.astype(F32)
                s[...] = v.astype(BF16)
            if phase == 1:
                def add(i, _):
                    total(self.at(kind, axis, me, i, mine), [self.rx1[k, i, every, :] for k in range(3)])
                    return 0
                lax.fori_loop(0, 4, add, 0)
            else:
                total(self.at(kind, axis, me, getattr(self, "xz"[h]), mine), [self.rx2[k, every, :] for k in range(3)])
        for _, cp, _ in hops:
            cp.wait_send()

    def step(self, i, kind, l):
        if i == 1:
            n, _, _, r = KINDS[kind]
            own, c = self.own[kind], self.c
            cc = self.c_copy(kind, l)
            cc.wait_recv()

            def add(i, _):
                z, x = i // 4, lax.rem(i, 4)
                own[c, z, x] = (own[c, z, x].astype(F32) + self.rc[z, x, r:r + n, :].astype(F32)).astype(BF16)
                return 0
            lax.fori_loop(0, 16, add, 0)

            @pl.when(l == 1)
            def _():
                pl.semaphore_signal(self.credit.at[kind], inc=1, device_id=self.dev("c", 1 - c), device_id_type=MESH)
            self.launch(kind, l, 1)
            cc.wait_send()
        elif i == 2:
            self.land(kind, l, 1)
            self.launch(kind, l, 2)
        else:
            self.land(kind, l, 2)
            n = KINDS[kind][0]
            _, every = self.rows(kind, l, 0, n)
            self.G[self.y, every, :] = self.own[kind][self.c, self.z, self.x]
            for o, there, _ in self.others("y"):
                self.y_copy(kind, l, o, self.y, there).start()

    def y_copy(self, kind, l, o, slot, there):
        _, every = self.rows(kind, l, 0, KINDS[kind][0])
        part = self.G.at[slot, every, :]
        return self.copy(part, part, (self.unit(kind, l), 3, there), self.dev("y", o))

    def y_done(self, kind, l):
        for o, there, here in self.others("y"):
            self.y_copy(kind, l, o, o, here).wait_recv()
            self.y_copy(kind, l, o, self.y, there).wait_send()

    def vec(self, b):
        return self.vecs[0].at[self.y] if b == 0 else self.vecs[b]

    def v_copy(self, b, stage, o, there):
        i = (0, 1, 4, 7)[stage] + there
        src = self.vec(b)
        dst = self.vxs[b].at[i]
        return pltpu.make_async_remote_copy(src_ref=src, dst_ref=dst, send_sem=self.vsems.at[b, i], recv_sem=self.vsemr.at[b, i],
                                            device_id=self.dev("cxzy"[stage], o), device_id_type=MESH)

    def v_start(self, b, stage):
        if stage:
            self.v_finish(b, stage - 1)
        for o, there, _ in self.others("cxzy"[stage]):
            self.v_copy(b, stage, o, there).start()

    def v_finish(self, b, stage):
        axis = "cxzy"[stage]
        me = getattr(self, axis)
        vec, vx = self.vec(b), self.vxs[b]
        for o, there, here in self.others(axis):
            self.v_copy(b, stage, o, here).wait_recv()
            self.v_copy(b, stage, o, there).wait_send()
            if b == 0 and stage == 3:
                self.vecs[0][o] = vx[7 + here]
        if b == 0 and stage == 3:
            return
        if stage == 0:
            vec[...] = vec[...] + vx[0]
            return
        own = vec[...]
        terms = []
        for p in range(4):
            slot = lax.rem(p - me + 7, 4)
            terms.append(jnp.where(slot == 3, own, vx[(1, 4, 7)[stage - 1] + jnp.minimum(slot, 2)]))
        vec[...] = (terms[0] + terms[1]) + (terms[2] + terms[3])


def head_block(h):
    k = h % 6
    if isinstance(h, int):
        return h // 6, slice(MB * (k // 3), MB * (k // 3) + MB), slice(MB * (k % 3), MB * (k % 3) + MB)
    return h // 6, pl.ds(pl.multiple_of(MB * (k // 3), MB), MB), pl.ds(pl.multiple_of(MB * (k % 3), MB), MB)


def chain(tok, cot, pages, bucket, ag, ash, win, qb, vb, tab, wout, ob, asc, fg, fsh, wup, ub, wdn, db, fsc,
       so, go, G, v0, v2, v3, e_st, af_st, dg_st,
       xs, low, qkv, E, mixed, br, af, dg, w_in, w_out, w_up, w_dn, T, AB, Dsc, bsc, fch, ach,
       rc, rx1, rx2, vx0, vx2, vx3, sem, sems, semr, vsems, vsemr, credit):
    cm = Comm((v0, v2, v3), fch, ach, rc, rx1, rx2, G, (vx0, vx2, vx3), sems, semr, vsems, vsemr, credit)
    y = cm.y
    def cp(src, dst, i):
        return pltpu.make_async_copy(src, dst, sem.at[i])
    def ldA(l):
        return [cp(win.at[l], w_in, 0), cp(wout.at[l], w_out, 1)]
    def ldF(l):
        return [cp(wup.at[l], w_up, 2), cp(wdn.at[l], w_dn, 3)]
    def start(cs):
        for c in cs: c.start()
    def wait(cs):
        for c in cs: c.wait()
    ctok = cp(tok, xs.at[0], 4)
    ccot = cp(cot, xs.at[5], 5)
    ctok.start()
    start(ldA(0))
    start(ldF(0))
    ccot.start()
    cm.signal_all()
    bsc[...] = jnp.full((1, 512), -1, jnp.int32)
    bsc[:, :511] = bucket[...]
    lane = lax.broadcasted_iota(jnp.int32, (1, 128), 1)
    m0 = (lane < 64).astype(F32).astype(BF16)
    m1 = (lane >= 64).astype(F32).astype(BF16)
    lanef = lax.broadcasted_iota(jnp.int32, (MB, 128), 1).astype(F32)
    for mb in range(2):
        pf = jnp.broadcast_to(pages[mb:mb + 1, :].astype(F32), (128, MB)).T
        same = pf == lanef
        AB[0, mb] = jnp.where(same | (lanef > 7.5), 0.0, -1e30).astype(BF16)
        AB[1, mb] = jnp.where(same, 1.0, 0.0).astype(BF16)
    turn = (lax.broadcasted_iota(jnp.int32, (512, 512), 0) + lax.broadcasted_iota(jnp.int32, (512, 512), 1) == 510).astype(F32).astype(BF16)
    turned = dot(jnp.broadcast_to(bsc[...].astype(F32), (16, 512)).astype(BF16), turn)[0:1, :]
    turned = jnp.where(lax.broadcasted_iota(jnp.int32, (1, 512), 1) == 511, -1.0, turned)
    sel = (lax.broadcasted_iota(jnp.int32, (NB, 512), 0).astype(F32) == turned).astype(F32)

    def layernorm(s, gain, shift):
        def body(i, _):
            r = pl.ds(pl.multiple_of(i * 64, 64), 64)
            x = xs[s, r, :].astype(F32)
            c = x - jnp.mean(x, -1, keepdims=True)
            n = c * lax.rsqrt(jnp.mean(c * c, -1, keepdims=True) + EPS)
            low[s, r, :] = (n * gain + shift).astype(BF16)
            return 0
        lax.fori_loop(0, R // 64, body, 0, unroll=UL)

    def residual(s, val, bias, scale):
        b = val + bias
        br[s] = b.astype(BF16)
        xs[s + 1] = (xs[s].astype(F32) + scale * b).astype(BF16)

    def masks(g, mb, l):
        rows = pl.ds(pl.multiple_of(mb * MB, MB), MB)
        c = pl.multiple_of(g * 128, 128)
        q = qkv[l, rows, pl.ds(c, 128)]
        k = qkv[l, rows, pl.ds(D + c, 128)]
        v = qkv[l, rows, pl.ds(2 * D + c, 128)]
        km = jnp.concatenate([k * m0, k * m1], 0)
        vm = jnp.concatenate([v * m0, v * m1], 0)
        return rows, pl.ds(c, 128), q, km, vm

    def attn_fwd(l):
        s = 2 * l
        row = lambda ref: ref[pl.ds(l, 1), :]
        obias = lax.dot_general(tab[:, pl.ds(l, 1), :].reshape(H, NB), sel, (((1,), (0,)), ((), ())), precision=lax.Precision.HIGHEST, preferred_element_type=F32)
        def toep():
            base = [pltpu.roll(jnp.broadcast_to(obias[h:h + 1, :], (8, 512)), 257, 1, stride=1, stride_axis=0) for h in range(H)]
            base = jnp.concatenate(base, 0)
            for a in range(MB // 8):
                t = pltpu.roll(base, 8 * a, 1) if a else base
                for h in range(H):
                    p, r, c = head_block(h)
                    T[p, r.start + 8 * a:r.start + 8 * a + 8, c] = t[8 * h:8 * h + 8, :MB]
        with jax.named_scope('toep'):
            toep()
        layernorm(s, row(ag), row(ash))
        x = low[s]
        qkv[l, :, 0:D] = ((dot(x, w_in[:, 0:D]) + row(qb)) * 0.125).astype(BF16)
        qkv[l, :, D:2 * D] = dot(x, w_in[:, D:2 * D]).astype(BF16)
        qkv[l, :, 2 * D:3 * D] = (dot(x, w_in[:, 2 * D:3 * D]) + row(vb)).astype(BF16)
        def pair(it, _):
            mb, g = it // 6, it % 6
            rows, cols, q, km, vm = masks(g, mb, l)
            qx = jnp.concatenate([q, AB[0, mb]], 1)
            kx = jnp.concatenate([km, jnp.concatenate([AB[1, mb]] * 2, 0)], 1)
            sc = dot_rt(kx, qx)
            def soft(v):
                e = jnp.exp(v - jnp.max(v, 0, keepdims=True))
                return e * (1.0 / jnp.sum(e, 0, keepdims=True))
            e = jnp.concatenate([soft(sc[:MB] + T[head_block(2 * g)]), soft(sc[MB:] + T[head_block(2 * g + 1)])], 0).astype(BF16)
            E[it] = e
            mixed[l, rows, cols] = dot_lt(vm, e).T.astype(BF16)
            return 0
        with jax.named_scope('pairs'):
            lax.fori_loop(0, 12, pair, 0, unroll=UP)
        residual(s, dot(mixed[l], w_out[...]), row(ob), row(asc))

    def ff_fwd(l):
        s = 2 * l + 1
        row = lambda ref: ref[pl.ds(l, 1), :]
        layernorm(s, row(fg), row(fsh))
        x = low[s]
        for j in range(4):
            u = dot(x, w_up[:, D * j:D * (j + 1)]) + ub[pl.ds(l, 1), D * j:D * (j + 1)]
            u2 = u * u
            t = jnp.tanh(u * (C0 + C1 * u2))
            h = 0.5 * t + 0.5
            af[:, D * j:D * (j + 1)] = (u * h).astype(BF16)
            dg[:, D * j:D * (j + 1)] = (h + (0.5 - 0.5 * t * t) * (u * (C0 + (3 * C1) * u2))).astype(BF16)
        for j in range(2):
            r = slice(256 * j, 256 * j + 256)
            b = dot(af[r], w_dn[...]) + row(db)
            br[s, r] = b.astype(BF16)
            xs[s + 1, r] = (xs[s, r].astype(F32) + row(fsc) * b).astype(BF16)

    def fwd(l, _):
        @pl.when(l == 1)
        def _():
            wait([cp(E, e_st, 6)])
        wait(ldA(l))
        attn_fwd(l)
        @pl.when(l == 0)
        def _():
            start(ldA(1))
            cp(E, e_st, 6).start()
        @pl.when(l == 1)
        def _():
            wait([cp(af, af_st, 7), cp(dg, dg_st, 8)])
        wait(ldF(l))
        ff_fwd(l)
        @pl.when(l == 0)
        def _():
            start(ldF(1))
            start([cp(af, af_st, 7), cp(dg, dg_st, 8)])
        return 0

    ctok.wait()
    lax.fori_loop(0, 2, fwd, 0)
    c_so = cp(xs.at[y + 1], so, 9)
    c_so.start()
    ccot.wait()
    cm.wait_all()

    def up_slot(s):
        return jnp.where(s == 3, 5, s + 1)

    def head_back(s, scale):
        us = up_slot(s)

        def body(i, c):
            a, b = c
            r = pl.ds(pl.multiple_of(i * 64, 64), 64)
            u = xs[us, r, :].astype(F32)
            g = (u * scale).astype(BF16)
            b8 = fold8(u * br[s, r, :].astype(F32))
            br[s, r, :] = g
            return a + b8, b + fold8(g.astype(F32))
        z = jnp.zeros((8, D), F32)
        a, b = lax.fori_loop(0, R // 64, body, (z, z), unroll=UL)
        return rowsum(a), rowsum(b)

    def tail_back(s, gain):
        us = up_slot(s)

        def body(i, c):
            a, b = c
            r = pl.ds(pl.multiple_of(i * 64, 64), 64)
            x = xs[s, r, :].astype(F32)
            gl = T[0, r, :]
            ce = x - jnp.mean(x, -1, keepdims=True)
            rs = lax.rsqrt(jnp.mean(ce * ce, -1, keepdims=True) + EPS)
            n = ce * rs
            gn = gl * n
            t = gl * gain
            u = xs[us, r, :].astype(F32)
            o = u + rs * (t - jnp.mean(t, -1, keepdims=True) - n * jnp.mean(t * n, -1, keepdims=True))
            xs[s, r, :] = o.astype(BF16)
            return a + fold8(gn), b + fold8(gl)
        z = jnp.zeros((8, D), F32)
        a, b = lax.fori_loop(0, R // 64, body, (z, z), unroll=UL)
        @pl.when(y == s)
        def _():
            cp(xs.at[s], go, 10).start()
        return rowsum(a), rowsum(b)

    def put_rows(dst, b, val, nb):
        for o in range(16):
            zz, xx, cc = o // 8, (o // 2) % 4, o % 2
            rows = val[24 * o:24 * o + 24, :]
            chunk = jnp.concatenate([rows[:, 384 * k:384 * (k + 1)] for k in range(nb)], 0)
            dst[cc, 2 * b + zz, xx] = chunk.astype(BF16)

    def ff_bwd(l):
        s = 2 * l + 1
        row = lambda ref: ref[pl.ds(l, 1), :]
        sg, dbg = head_back(s, row(fsc))
        v0[l, 3:4, :] = sg
        v0[l, 2:3, :] = dbg
        g = br[s]
        for j in range(4):
            c = slice(D * j, D * (j + 1))
            ga = dot_rt(g, w_dn[c, :])
            gbef = (ga * dg[:, c].astype(F32)).astype(BF16)
            dg[:, c] = gbef
            v0[l, 4 + j:5 + j, :] = rowsum(fold8(gbef.astype(F32)))
        @pl.when(l == 0)
        def _():
            cm.step(3, 0, 1)
        @pl.when(y < 2)
        def _():
            def b2(b, _):
                a = low[s, :, pl.ds(pl.multiple_of(b * 384, 128), 384)]
                put_rows(fch, b, dot_lt(a, dg[:, pl.ds(pl.multiple_of(y * 1536, 128), 1536)]), 4)
                return 0
            lax.fori_loop(0, 2, b2, 0)
        @pl.when(y >= 2)
        def _():
            gq = br[s, :, pl.ds(pl.multiple_of((y - 2) * 384, 128), 384)]
            def b4(zz, _):
                a = af[:, pl.ds(pl.multiple_of(zz * 768, 128), 768)]
                val = dot_lt(a, gq).astype(BF16)
                for o in range(8):
                    fch[o % 2, zz, o // 2] = val[96 * o:96 * o + 96, :]
                return 0
            lax.fori_loop(0, 4, b4, 0)
        cm.c_start(0, l)
        for j in range(2):
            T[0, 256 * j:256 * j + 256] = dot_rt(dg[256 * j:256 * j + 256], w_up[...])
        @pl.when(l == 0)
        def _():
            cm.step(2, 1, 1)
        @pl.when(l == 1)
        def _():
            c_so.wait()
        gg, sh = tail_back(s, row(fg))
        v0[l, 0:1, :] = gg
        v0[l, 1:2, :] = sh

    def attn_bwd(l):
        s = 2 * l
        row = lambda ref: ref[pl.ds(l, 1), :]
        sg, obg = head_back(s, row(asc))

        def small(i, val):
            @pl.when(l == 1)
            def _():
                v0[2, i:i + 1, :] = val
            @pl.when(l == 0)
            def _():
                if i < 2:
                    v2[i:i + 1, :] = val
                else:
                    v0[3, i:i + 1, :] = val
        small(5, sg)
        small(4, obg)
        cm.step(1, 0, l)
        low[s + 1] = dot_rt(br[s], w_out[...]).astype(BF16)
        T[...] = jnp.zeros_like(T)

        def pair(mb, g):
            it = 6 * mb + g
            rows, cols, q, km, vm = masks(g, mb, l)
            dop = low[s + 1, rows, cols]
            dp = dot_rt(vm, dop)
            e = E[it]
            ef = e.astype(F32)
            pt = ef * dp
            in0 = jnp.sum(pt[:MB], 0, keepdims=True) / jnp.sum(ef[:MB], 0, keepdims=True)
            in1 = jnp.sum(pt[MB:], 0, keepdims=True) / jnp.sum(ef[MB:], 0, keepdims=True)
            ds = jnp.concatenate([pt[:MB] - ef[:MB] * in0, pt[MB:] - ef[MB:] * in1], 0).astype(BF16)
            for k in range(2):
                b = head_block(2 * g + k)
                T[b] = T[b] + ds[MB * k:MB * k + MB].astype(F32)
            dv = dot(e, dop)
            dk = dot(ds, q)
            dq = (dot_lt(km, ds) * 0.125).T
            hm = lane < 64
            c0 = pl.multiple_of(g * 128, 128)
            qkv[l, rows, pl.ds(c0, 128)] = dq.astype(BF16)
            qkv[l, rows, pl.ds(D + c0, 128)] = jnp.where(hm, dk[:MB], dk[MB:]).astype(BF16)
            qkv[l, rows, pl.ds(2 * D + c0, 128)] = jnp.where(hm, dv[:MB], dv[MB:]).astype(BF16)

        def half(mb, _):
            for g in range(6):
                pair(mb, g)
            @pl.when((mb == 0) & (l == 0))
            def _():
                cm.step(3, 1, 1)
            return 0
        lax.fori_loop(0, 2, half, 0)
        def cs(i, c):
            a, b = c
            r = pl.ds(pl.multiple_of(i * 64, 64), 64)
            return a + fold8(qkv[l, r, 0:D].astype(F32)), b + fold8(qkv[l, r, 2 * D:3 * D].astype(F32))
        z = jnp.zeros((8, D), F32)
        a, b = lax.fori_loop(0, R // 64, cs, (z, z), unroll=UL)
        small(2, rowsum(a))
        small(3, rowsum(b))
        @pl.when(l == 0)
        def _():
            cm.v_start(0, 0)
        @pl.when(y < 3)
        def _():
            def b2(b, _):
                a = low[s, :, pl.ds(pl.multiple_of(b * 384, 128), 384)]
                put_rows(ach, b, dot_lt(a, qkv[l, :, pl.ds(pl.multiple_of(y * D, 128), D)]), 2)
                return 0
            lax.fori_loop(0, 2, b2, 0)
        @pl.when(y == 3)
        def _():
            def b2(b, _):
                a = mixed[l, :, pl.ds(pl.multiple_of(b * 384, 128), 384)]
                put_rows(ach, b, dot_lt(a, br[s]), 2)
                return 0
            lax.fori_loop(0, 2, b2, 0)
        cm.c_start(1, l)
        def fo(h, _):
            h = 3 * y + h
            a = T[head_block(h)]
            a = jnp.concatenate([a, jnp.zeros((MB, MB), F32)], 1)
            n = MB // 2
            while n >= 1:
                a = a[n:, :] + pltpu.roll(a[:n, :], n, 1)
                n //= 2
            Dsc[pl.ds(h, 1), :] = a
            return 0
        with jax.named_scope('fold'):
            lax.fori_loop(0, 3, fo, 0, unroll=True)
        tg = lax.dot_general(Dsc[...], sel, (((1,), (1,)), ((), ())), precision=lax.Precision.HIGHEST, preferred_element_type=F32)
        v3[pl.ds(pl.multiple_of(l * 16, 16), 16), :] = jnp.concatenate([tg, jnp.zeros((16, 96), F32)], 1)
        @pl.when(l == 0)
        def _():
            cm.v_start(2, 0)
            cm.v_start(0, 1)
        T[0] = dot_rt(qkv[l], w_in[...])
        cm.step(1, 1, l)
        @pl.when(l == 0)
        def _():
            cm.v_start(2, 1)
        cm.step(2, 0, l)
        gg, sh = tail_back(s, row(ag))
        small(0, gg)
        small(1, sh)

    v0[...] = jnp.zeros_like(v0)
    Dsc[...] = jnp.zeros_like(Dsc)

    def bwd(i, _):
        l = 1 - i
        @pl.when(l == 0)
        def _():
            wait(ldF(0))
            wait([cp(af_st, af, 7), cp(dg_st, dg, 8)])
        ff_bwd(l)
        @pl.when(l == 1)
        def _():
            start(ldF(0))
            start([cp(af_st, af, 7), cp(dg_st, dg, 8)])
        @pl.when(l == 0)
        def _():
            wait(ldA(0))
            wait([cp(e_st, E, 6)])
        attn_bwd(l)
        @pl.when(l == 1)
        def _():
            start(ldA(0))
            cp(e_st, E, 6).start()
        return 0
    lax.fori_loop(0, 2, bwd, 0)
    cm.v_start(1, 0)
    cm.v_start(0, 2)
    cm.v_start(2, 2)
    cm.v_start(1, 1)
    cm.step(2, 1, 0)
    cm.step(3, 0, 0)
    cm.v_start(0, 3)
    cm.v_start(2, 3)
    cm.v_start(1, 2)
    cm.step(3, 1, 0)
    cm.v_finish(0, 3)
    cm.v_finish(2, 3)
    cm.v_finish(1, 2)
    cp(xs.at[y], go, 10).wait()
    for l in (1, 0):
        for k in range(2):
            cm.y_done(k, l)


def run_chain(tokens, cotangent, pages, bucket, ag, ash, win, qb, vb, tab, wout, ob, asc, fg, fsh, wup, ub, wdn, db, fsc):
    tok = tokens.reshape(R, D)
    cot = cotangent.reshape(R, D)
    bucket = bucket.reshape(1, 511)
    tab = jnp.transpose(tab, (1, 0, 2))
    ANY = pl.BlockSpec(memory_space=pl.ANY)
    V = pl.BlockSpec(memory_space=pltpu.VMEM)
    sds = jax.ShapeDtypeStruct
    outs = (sds((R, D), BF16), sds((R, D), BF16), sds((4, 288, 384), BF16), sds((4, 8, D), F32), sds((2, D), F32), sds((32, 128), F32),
            sds((12, 512, MB), BF16), sds((R, FF), BF16), sds((R, FF), BF16))
    vm = pltpu.VMEM
    S = pltpu.SemaphoreType.DMA
    scratch = [
        vm((6, R, D), BF16), vm((4, R, D), BF16), vm((2, R, 3 * D), BF16), vm((12, 512, MB), BF16),
        vm((2, R, D), BF16), vm((4, R, D), BF16), vm((R, FF), BF16), vm((R, FF), BF16),
        vm((D, 3 * D), BF16), vm((D, D), BF16), vm((D, FF), BF16), vm((FF, D), BF16),
        vm((2, R, D), F32),
        vm((2, 2, MB, 128), BF16), vm((16, 512), F32), vm((1, 512), jnp.int32), vm((2, 4, 4, 96, 384), BF16), vm((2, 4, 4, 48, 384), BF16),
        vm((4, 4, 144, 384), BF16), vm((3, 4, 288, 384), BF16), vm((3, 288, 384), BF16),
        vm((10, 8, D), F32), vm((7, 2, D), F32), vm((10, 32, 128), F32),
        S((11,)), S((4, 4, 6)), S((4, 4, 6)), S((3, 10)), S((3, 10)), pltpu.SemaphoreType.REGULAR((2,)),
    ]
    return pl.pallas_call(
        chain,
        out_shape=outs,
        in_specs=[ANY, ANY, V, V, V, V, ANY, V, V, V, ANY, V, V, V, V, ANY, V, ANY, V, V],
        out_specs=(ANY, ANY, V, V, V, V, ANY, ANY, ANY),
        scratch_shapes=scratch,
        compiler_params=pltpu.CompilerParams(vmem_limit_bytes=63400000, collective_id=0, has_side_effects=True),
        name="chain",
    )(tok, cot, pages, bucket, ag, ash, win, qb, vb, tab, wout, ob, asc, fg, fsh, wup, ub, wdn, db, fsc)


def unpack(so_in, go_in, G_in, v0_in, v2_in, v3_in, so, go, a_gain, a_shift, w_in, qb, vb, tab, w_out, ob, asc, fg, fsh, w_up, ub, w_dn, db, fsc, G, v0, v2, v3, so_mid, go_mid, sem):
    d = lax.axis_index("dp")
    pairs = ((G_in, G), (v0_in, v0), (v2_in, v2), (v3_in, v3), (so_in, so_mid), (go_in, go_mid))
    copies = [pltpu.make_async_copy(a, b, sem.at[i]) for i, (a, b) in enumerate(pairs)]
    for cp in copies:
        cp.start()
    for cp in copies[:4]:
        cp.wait()
    last = [pltpu.make_async_copy(a, b, sem.at[6 + i]) for i, (a, b) in enumerate(((so_mid, so), (go_mid, go)))]
    for a, b in zip(copies[4:], last):
        a.wait()
        b.start()
    for l in range(2):
        for y in range(4):
            f = G[y, 96 * l:96 * l + 96, :].astype(F32)
            a = G[y, 192 + 48 * l:240 + 48 * l, :].astype(F32)
            if y < 2:
                for k in range(4):
                    w_up[l, :, 1536 * y + 384 * k:1536 * y + 384 * (k + 1)] = f[24 * k:24 * k + 24]
            else:
                w_dn[l, :, 384 * (y - 2):384 * (y - 1)] = f
            for k in range(2):
                if y < 3:
                    w_in[l, :, 768 * y + 384 * k:768 * y + 384 * (k + 1)] = a[24 * k:24 * k + 24]
                else:
                    w_out[l, :, 384 * k:384 * (k + 1)] = a[24 * k:24 * k + 24]
    shift = lax.rem(D - 24 * d, D)
    r0 = [pltpu.roll(v0[i], shift, 1)[:, :128] for i in range(4)]
    r2 = pltpu.roll(jnp.concatenate([v2[...], jnp.zeros((6, D), F32)], 0), shift, 1)[:, :128]
    for i, ref in enumerate((fg, fsh, db, fsc)):
        for l in range(2):
            ref[l:l + 1, :] = r0[l][i:i + 1, :24]
    for i, ref in enumerate((a_gain, a_shift, qb, vb, ob, asc)):
        ref[1:2, :] = r0[2][i:i + 1, :24]
        ref[0:1, :] = (r2 if i < 2 else r0[3])[i:i + 1, :24]
    for l in range(2):
        row = v0[l, pl.ds(4 + d // 8, 1), :]
        ub[l:l + 1, :] = pltpu.roll(jnp.broadcast_to(row, (8, D)), lax.rem(D - 96 * lax.rem(d, 8), D), 1)[0:1, :96]
        tab[:, l, :] = v3[16 * l:16 * l + H, :NB]
    for cp in last:
        cp.wait()


def run_unpack(*args):
    V = pl.BlockSpec(memory_space=pltpu.VMEM)
    ANY = pl.BlockSpec(memory_space=pl.ANY)
    sds = jax.ShapeDtypeStruct
    w = sds((2, 24), F32)
    outs = (sds((R, D), BF16), sds((R, D), BF16), w, w, sds((2, 24, 2304), F32), w, w, sds((H, 2, NB), F32), sds((2, 24, D), F32), w, w, w, w,
            sds((2, 24, FF), F32), sds((2, 96), F32), sds((2, 96, D), F32), w, w)
    vm = pltpu.VMEM
    return pl.pallas_call(
        unpack, out_shape=outs, in_specs=[ANY] * 6, out_specs=(ANY, ANY) + (V,) * 16, name="unpack",
        scratch_shapes=[vm((4, 288, 384), BF16), vm((4, 8, D), F32), vm((2, D), F32), vm((32, 128), F32), vm((R, D), BF16), vm((R, D), BF16), pltpu.SemaphoreType.DMA((8,))],
        compiler_params=pltpu.CompilerParams(vmem_limit_bytes=63400000))(*args)


def body(*args):
    so, go, *outs = run_unpack(*run_chain(*args)[:6])
    outs[5] = jnp.transpose(outs[5], (1, 0, 2))
    return (so.reshape(1, 2, MB, D), go.reshape(1, 2, MB, D)) + tuple(outs)


def solution(mesh):
    data, whole = P("dp", None, None), P()
    w1, w2 = P(None, "dp"), P(None, "dp", None)
    return jax.shard_map(
        body,
        mesh=mesh,
        in_specs=(data, data, P("dp", None)) + (whole,) * 17,
        out_specs=(P("section", "dp", None, None),) * 2 + (w1, w1, w2, w1, w1, P(), w2, w1, w1, w1, w1, w2, w1, w2, w1, w1),
        check_vma=False,
    )
```

time: 136 us -> 113 us (0.83)
  Pallas kernels: 129 us -> 111 us
  local copies, waits for them, and re-layouts: 5.02 us -> 0 us
    pallas_call x1, Pallas kernels: 128 us -> 107 us  [run_chain(): pl.pallas_call(chain, out_shape=outs, in_specs=[ANY, ANY, V, V, V, V, ANY...]
    unnamed x8 -> x0, local copies, waits for them, and re-layouts: 5.02 us -> none
    pallas_call x1, Pallas kernels: 1.31 us -> 3.92 us  [run_unpack(): pl.pallas_call(unpack, out_shape=outs, in_specs=[ANY] * 6, out_specs=(ANY...]
where the time goes in v3:
time: 113 us; the launch traced here: 112 us
  Pallas kernels  111 us (98%)
    pallas_call x1, Pallas kernels, run_chain(): pl.pallas_call(chain, out_shape=outs, in_specs=[ANY, ANY, V, V, V, V, ANY...  107 us
    pallas_call x1, Pallas kernels, run_unpack(): pl.pallas_call(unpack, out_shape=outs, in_specs=[ANY] * 6, out_specs=(ANY...  3.92 us

profile of v3, /device:TPU:1, one launch (start us, length us, event | category | flops | bytes accessed | tf_op | source)
XLA Modules:
  0.0 111.8 jit_solution(8695277194323329338)
XLA Ops:
  0.7 107.1 %chain.1 = (bf16[512,768]{1,0:T(8,128)(2,1)}, bf16[512,768]{1,0:T(8,128)(2,1)}, bf16[4,288,384]{2,1,0:T(8,128)(2,1)}, f32[4,8,768]{2,1,0:T(8,128)}, f32[2,768]{1...) custom-call(bf16[512,768]{1,0:T(8,128)(2,1)} %bitcast.7, ...), custom_call_target="tpu_custom_call" | custom-call | tf_op jit(solution)/shard_map/chain/pallas_call | solution.py:644
  107.8 3.9 %unpack.1 = (bf16[512,768]{1,0:T(8,128)(2,1)}, bf16[512,768]{1,0:T(8,128)(2,1)}, f32[2,24]{1,0:T(2,128)}, f32[2,24]{1,0:T(2,128)}, f32[2,24,2304]{2,1,0:T(8,128)...) custom-call(bf16[512,768]{1,0:T(8,128)(2,1)} %get-tuple-element.42.s, ...), custom_call_target="tpu_custom_call" | custom-call | tf_op jit(solution)/shard_map/unpack/pallas_call | solution.py:706

commit v4 on v3

--- a/solution.py
+++ b/solution.py
@@ -513,14 +513,29 @@
             qkv[l, rows, pl.ds(D + c0, 128)] = jnp.where(hm, dk[:MB], dk[MB:]).astype(BF16)
             qkv[l, rows, pl.ds(2 * D + c0, 128)] = jnp.where(hm, dv[:MB], dv[MB:]).astype(BF16)
 
-        def half(mb, _):
-            for g in range(6):
-                pair(mb, g)
-            @pl.when((mb == 0) & (l == 0))
-            def _():
-                cm.step(3, 1, 1)
-            return 0
-        lax.fori_loop(0, 2, half, 0)
+        for g in range(6):
+            pair(0, g)
+
+        @pl.when(l == 0)
+        def _():
+            cm.step(3, 1, 1)
+        for g in range(6):
+            pair(1, g)
+        @pl.when(y < 3)
+        def _():
+            def b2(b, _):
+                a = low[s, :, pl.ds(pl.multiple_of(b * 384, 128), 384)]
+                put_rows(ach, b, dot_lt(a, qkv[l, :, pl.ds(pl.multiple_of(y * D, 128), D)]), 2)
+                return 0
+            lax.fori_loop(0, 2, b2, 0)
+        @pl.when(y == 3)
+        def _():
+            def b2(b, _):
+                a = mixed[l, :, pl.ds(pl.multiple_of(b * 384, 128), 384)]
+                put_rows(ach, b, dot_lt(a, br[s]), 2)
+                return 0
+            lax.fori_loop(0, 2, b2, 0)
+        cm.c_start(1, l)
         def cs(i, c):
             a, b = c
             r = pl.ds(pl.multiple_of(i * 64, 64), 64)
@@ -532,21 +547,6 @@
         @pl.when(l == 0)
         def _():
             cm.v_start(0, 0)
-        @pl.when(y < 3)
-        def _():
-            def b2(b, _):
-                a = low[s, :, pl.ds(pl.multiple_of(b * 384, 128), 384)]
-                put_rows(ach, b, dot_lt(a, qkv[l, :, pl.ds(pl.multiple_of(y * D, 128), D)]), 2)
-                return 0
-            lax.fori_loop(0, 2, b2, 0)
-        @pl.when(y == 3)
-        def _():
-            def b2(b, _):
-                a = mixed[l, :, pl.ds(pl.multiple_of(b * 384, 128), 384)]
-                put_rows(ach, b, dot_lt(a, br[s]), 2)
-                return 0
-            lax.fori_loop(0, 2, b2, 0)
-        cm.c_start(1, l)
         def fo(h, _):
             h = 3 * y + h
             a = T[head_block(h)]
@@ -654,16 +654,16 @@
 
 def unpack(so_in, go_in, G_in, v0_in, v2_in, v3_in, so, go, a_gain, a_shift, w_in, qb, vb, tab, w_out, ob, asc, fg, fsh, w_up, ub, w_dn, db, fsc, G, v0, v2, v3, so_mid, go_mid, sem):
     d = lax.axis_index("dp")
-    pairs = ((G_in, G), (v0_in, v0), (v2_in, v2), (v3_in, v3), (so_in, so_mid), (go_in, go_mid))
+    pairs = ((so_in, so_mid), (go_in, go_mid), (G_in, G), (v0_in, v0), (v2_in, v2), (v3_in, v3))
     copies = [pltpu.make_async_copy(a, b, sem.at[i]) for i, (a, b) in enumerate(pairs)]
     for cp in copies:
         cp.start()
-    for cp in copies[:4]:
-        cp.wait()
     last = [pltpu.make_async_copy(a, b, sem.at[6 + i]) for i, (a, b) in enumerate(((so_mid, so), (go_mid, go)))]
-    for a, b in zip(copies[4:], last):
+    for a, b in zip(copies[:2], last):
         a.wait()
         b.start()
+    for cp in copies[2:]:
+        cp.wait()
     for l in range(2):
         for y in range(4):
             f = G[y, 96 * l:96 * l + 96, :].astype(F32)

time: 113 us -> 110 us (0.973); the launches traced: 112 us -> 110 us
  Pallas kernels: 111 us -> 109 us
    pallas_call x1, Pallas kernels: 107 us -> 106 us  [run_chain(): pl.pallas_call(chain, out_shape=outs, in_specs=[ANY, ANY, V, V, V, V, ANY...]
where the time goes in v4:
time: 110 us
  Pallas kernels  109 us (99%)
    pallas_call x1, Pallas kernels, run_chain(): pl.pallas_call(chain, out_shape=outs, in_specs=[ANY, ANY, V, V, V, V, ANY...  106 us
    pallas_call x1, Pallas kernels, run_unpack(): pl.pallas_call(unpack, out_shape=outs, in_specs=[ANY] * 6, out_specs=(ANY...  3.59 us

profile of v4, /device:TPU:1, one launch (start us, length us, event | category | flops | bytes accessed | tf_op | source)
XLA Modules:
  0.0 110.2 jit_solution(13045630307798346327)
XLA Ops:
  0.7 105.8 %chain.1 = (bf16[512,768]{1,0:T(8,128)(2,1)}, bf16[512,768]{1,0:T(8,128)(2,1)}, bf16[4,288,384]{2,1,0:T(8,128)(2,1)}, f32[4,8,768]{2,1,0:T(8,128)}, f32[2,768]{1...) custom-call(bf16[512,768]{1,0:T(8,128)(2,1)} %bitcast.7, ...), custom_call_target="tpu_custom_call" | custom-call | tf_op jit(solution)/shard_map/chain/pallas_call | solution.py:644
  106.4 3.6 %unpack.1 = (bf16[512,768]{1,0:T(8,128)(2,1)}, bf16[512,768]{1,0:T(8,128)(2,1)}, f32[2,24]{1,0:T(2,128)}, f32[2,24]{1,0:T(2,128)}, f32[2,24,2304]{2,1,0:T(8,128)...) custom-call(bf16[512,768]{1,0:T(8,128)(2,1)} %get-tuple-element.42.s, ...), custom_call_target="tpu_custom_call" | custom-call | tf_op jit(solution)/shard_map/unpack/pallas_call | solution.py:706

commit v5 on v4

--- a/solution.py
+++ b/solution.py
@@ -565,8 +565,11 @@
         def _():
             cm.v_start(2, 0)
             cm.v_start(0, 1)
+            cm.step(1, 1, 0)
         T[0] = dot_rt(qkv[l], w_in[...])
-        cm.step(1, 1, l)
+        @pl.when(l == 1)
+        def _():
+            cm.step(1, 1, 1)
         @pl.when(l == 0)
         def _():
             cm.v_start(2, 1)

time: 110 us -> 109 us (level)
    pallas_call x1, Pallas kernels: 106 us -> 104 us  [run_chain(): pl.pallas_call(chain, out_shape=outs, in_specs=[ANY, ANY, V, V, V, V, ANY...]
where the time goes in v5:
time: 109 us
  Pallas kernels  108 us (99%)
    pallas_call x1, Pallas kernels, run_chain(): pl.pallas_call(chain, out_shape=outs, in_specs=[ANY, ANY, V, V, V, V, ANY...  104 us
    pallas_call x1, Pallas kernels, run_unpack(): pl.pallas_call(unpack, out_shape=outs, in_specs=[ANY] * 6, out_specs=(ANY...  3.59 us

profile of v5, /device:TPU:1, one launch (start us, length us, event | category | flops | bytes accessed | tf_op | source)
XLA Modules:
  0.0 108.8 jit_solution(10823261601325808676)
XLA Ops:
  0.7 104.4 %chain.1 = (bf16[512,768]{1,0:T(8,128)(2,1)}, bf16[512,768]{1,0:T(8,128)(2,1)}, bf16[4,288,384]{2,1,0:T(8,128)(2,1)}, f32[4,8,768]{2,1,0:T(8,128)}, f32[2,768]{1...) custom-call(bf16[512,768]{1,0:T(8,128)(2,1)} %bitcast.7, ...), custom_call_target="tpu_custom_call" | custom-call | tf_op jit(solution)/shard_map/chain/pallas_call | solution.py:647
  105.0 3.6 %unpack.1 = (bf16[512,768]{1,0:T(8,128)(2,1)}, bf16[512,768]{1,0:T(8,128)(2,1)}, f32[2,24]{1,0:T(2,128)}, f32[2,24]{1,0:T(2,128)}, f32[2,24,2304]{2,1,0:T(8,128)...) custom-call(bf16[512,768]{1,0:T(8,128)(2,1)} %get-tuple-element.42.s, ...), custom_call_target="tpu_custom_call" | custom-call | tf_op jit(solution)/shard_map/unpack/pallas_call | solution.py:709
